TPU v7x, 512 devices: a whole 4x8x8 slice. The times are simulated.
512 devices in a mesh: sample: 32 (over x_lo, y, core), feat: 16 (over z, x_hi).
Axes of the slice: x: 4 (x_hi: 2, x_lo: 2; x = x_hi * 2 + x_lo), y: 8, z: 8, core: 2. Of those that a mesh axis runs over, the one named last changes fastest.
Arguments:
- features: bfloat16 [131072, 4096], P('sample', 'feat'), may hold values from -6 to 6
- pre_one: bfloat16 [131072, 512], P(('sample', 'feat')), may hold values from -6 to 6
- pre_two: bfloat16 [131072, 512], P(('sample', 'feat')), may hold values from -6 to 6
- cotangent: bfloat16 [65536, 512], P(('sample', 'feat')), may hold values from -0.25 to 0.25
- weight_two: bfloat16 [512, 512], replicated, may hold values from -0.25 to 0.25
- weight_three: bfloat16 [512, 512], replicated, may hold values from -0.25 to 0.25
- lists_one: int32 [131072, 15], P('sample'), may hold values from 0 to 255
- degree_one: int32 [131072], P('sample'), may hold values from 1 to 15
- lists_two: int32 [131072, 10], P(('sample', 'feat')), may hold values from 0 to 255
- degree_two: int32 [131072], P(('sample', 'feat')), may hold values from 1 to 10
- lists_three: int32 [65536, 5], P(('sample', 'feat')), may hold values from 0 to 255
- degree_three: int32 [65536], P(('sample', 'feat')), may hold values from 1 to 5
Outputs:
- grad_one: float32 [4096, 512], P('feat')
- grad_two: float32 [512, 512], P('sample')
- grad_three: float32 [512, 512], P('sample')
All inputs are finite; a program needn't handle non-finite values.
Results may differ from a plain program's by a relative error of at most 0.006.
Values may be sent and summed in bfloat16 or wider, within the bound.
No kernel may reach another device: no remote copies, remote signals or barrier semaphores. Data moves between devices by JAX's collectives and lax.ppermute only.
A program may use at most 64 MiB of HBM per device.

v0:
```python
import jax
import jax.numpy as jnp
from jax import lax
from jax.sharding import PartitionSpec as P

NODES = 256


def count_tiles(neighbor_rows, degrees, width):
    columns = jnp.arange(width, dtype=jnp.int32)
    total = jnp.zeros((neighbor_rows.shape[0], width), jnp.float32)
    for column in range(neighbor_rows.shape[1]):
        hit = (neighbor_rows[:, column : column + 1] == columns[None, :]) & (
            column < degrees[:, None]
        )
        total = total + hit.astype(jnp.float32)
    return total.astype(jnp.bfloat16)


def contract_rows(left, right):
    return lax.dot_general(
        left, right, (((0,), (0,)), ((), ())), preferred_element_type=jnp.float32
    )


def deep_layers(
    pre_one,
    pre_two,
    cotangent,
    weight_two,
    weight_three,
    lists_two,
    degree_two,
    lists_three,
    degree_three,
):
    hidden_two = jnp.maximum(pre_two, jnp.zeros_like(pre_two))
    hidden_one = jnp.maximum(pre_one, jnp.zeros_like(pre_one))
    tile_three = count_tiles(lists_three, degree_three, pre_two.shape[0])
    scale_three = degree_three.astype(jnp.float32)[:, None]
    mean_three = (
        jnp.dot(tile_three, hidden_two, preferred_element_type=jnp.float32) / scale_three
    ).astype(jnp.bfloat16)
    term_three = contract_rows(mean_three, cotangent)
    back_three = (
        jnp.dot(cotangent, weight_three.T, preferred_element_type=jnp.float32) / scale_three
    ).astype(jnp.bfloat16)
    delta_two = jnp.where(pre_two > 0, contract_rows(tile_three, back_three), 0.0).astype(
        jnp.bfloat16
    )
    tile_two = count_tiles(lists_two, degree_two, pre_one.shape[0])
    scale_two = degree_two.astype(jnp.float32)[:, None]
    mean_two = (
        jnp.dot(tile_two, hidden_one, preferred_element_type=jnp.float32) / scale_two
    ).astype(jnp.bfloat16)
    term_two = contract_rows(mean_two, delta_two)
    back_two = (
        jnp.dot(delta_two, weight_two.T, preferred_element_type=jnp.float32) / scale_two
    ).astype(jnp.bfloat16)
    delta_one = jnp.where(pre_one > 0, contract_rows(tile_two, back_two), 0.0).astype(jnp.bfloat16)
    return (delta_one, term_two, term_three)


def body(
    features,
    pre_one,
    pre_two,
    cotangent,
    weight_two,
    weight_three,
    lists_one,
    degree_one,
    lists_two,
    degree_two,
    lists_three,
    degree_three,
):
    delta_one, term_two, term_three = deep_layers(
        pre_one,
        pre_two,
        cotangent,
        weight_two,
        weight_three,
        lists_two,
        degree_two,
        lists_three,
        degree_three,
    )
    feat_width = features.shape[1]
    piece = lax.all_gather(delta_one, "feat", axis=0, tiled=True)
    row_count = piece.shape[0]
    group_count = row_count // NODES
    tile = count_tiles(lists_one, degree_one, NODES).reshape(group_count, NODES, NODES)
    summed = jnp.einsum(
        "mij,mjc->mic",
        tile,
        features.reshape(group_count, NODES, feat_width),
        preferred_element_type=jnp.float32,
    ).reshape(row_count, feat_width)
    mean_one = (summed / degree_one.astype(jnp.float32)[:, None]).astype(jnp.bfloat16)
    folded = contract_rows(mean_one, piece)
    grad_one = lax.psum(folded, "sample")
    share = term_two.shape[0] // lax.axis_size("sample")
    total_two, total_three = lax.psum((term_two, term_three), ("sample", "feat"))
    offset = lax.axis_index("sample") * share
    grad_two = lax.dynamic_slice_in_dim(total_two, offset, share, 0)
    grad_three = lax.dynamic_slice_in_dim(total_three, offset, share, 0)
    return (grad_one, grad_two, grad_three)


def solution(mesh):
    return jax.shard_map(
        body,
        mesh=mesh,
        in_specs=(
            P("sample", "feat"),
            P(("sample", "feat"), None),
            P(("sample", "feat"), None),
            P(("sample", "feat"), None),
            P(),
            P(),
            P("sample", None),
            P("sample"),
            P(("sample", "feat"), None),
            P(("sample", "feat")),
            P(("sample", "feat"), None),
            P(("sample", "feat")),
        ),
        out_specs=(P("feat", None), P("sample", None), P("sample", None)),
        check_vma=False,
    )
```

profile of v0, /device:TPU:1, one launch (start us, length us, event | category | flops | bytes accessed | tf_op | source)
XLA Modules:
  0.0 565.0 jit_solution(6939772060377958602)
XLA Ops:
  8.0 0.0 copy-start
  8.0 0.0 all-gather.2.cloned.1.call-start
  8.1 0.8 broadcast_compare_fusion.29
  8.9 0.7 convert_element_type.180
  9.5 0.7 broadcast_compare_fusion.24
  10.2 0.7 convert_element_type.183
  10.9 0.9 slice_bitcast_fusion.4
  11.8 1.0 fusion.86
  12.8 0.0 copy-start.3
  12.8 0.0 copy-start.5
  12.8 1.7 fusion.49
  14.5 0.0 copy-start.4
  14.5 3.0 fusion.50
  17.5 0.0 all-gather.2.cloned.1.call-update
  17.5 0.0 copy-start.2
  17.5 0.0 copy-start.1
  17.5 0.0 all-reduce.6.cloned.1.call-start
  17.6 0.0 copy-done.3
  17.6 0.0 copy-done.5
  17.6 1.6 fusion.54
  19.2 0.0 copy-done.4
  19.2 2.3 fusion.51
  21.5 0.0 all-reduce.6.cloned.1.call-update
  21.5 0.0 all-reduce.4.cloned.1.call-start
  21.6 0.0 copy-done.2
  21.6 0.0 copy-done.1
  21.6 0.6 slice_reduce_fusion.14
  22.8 17.8 %add_convert_fusion.12 = bf16[16,256,256]{2,1,0:T(8,128)(2,1)S(1)} fusion(s32[16,256]{1,0:T(8,128)S(1)} %eq.521, s32[16,256]{1,0:T(8,128)S(1)} %eq.517, s32[16,256]{1,0:T(8,128)S(1)} %eq.513, s32[16,256]{1,0:T(8,128)S(1)} %eq.509, s32[16,256]{1,0:T(8,128)S(1)} %eq.505, s32[16,256]{1,0:T(8,128)S(1)} %eq.501, s32[16,256]{1,0:T(8,128)S(1)} %eq.497, ...), kind=kLoop, calls=%fused_computation.2.clone.clone.1 | loop fusion | flops 62914560 | bytes 2404352 | tf_op jit(solution)/shard_map/mij,mjc->mic/dot_general | solution.py:94
  40.5 0.0 copy-done
  40.5 0.7 fusion.16
  41.3 2.0 fusion
  43.3 82.8 %all-gather.2.cloned.1.call-done = bf16[4096,512]{1,0:T(8,128)(2,1)} async-done(((bf16[256,512]{1,0:T(8,128)(2,1)}), bf16[4096,512]{1,0:T(8,128)(2,1)}) %all-gather.2.cloned.1.call-update) | async-done | bytes 4194320 | tf_op jit(solution)/shard_map/all_gather | solution.py:90
  126.1 4.9 fusion.87
  131.0 0.0 all-reduce.4.cloned.1.call-update
  131.1 198.1 %all-reduce.6.cloned.1.call-done = (f32[512,512]{1,0:T(8,128)}, f32[512,512]{1,0:T(8,128)}) async-done(((f32[512,512]{1,0:T(8,128)}, f32[512,512]{1,0:T(8,128)}), (f32[512,512]{1,0:T(8,128)}, f32[512,512]{1,0:T(8,128)})) %all-reduce.6.cloned.1.call-update) | async-done | bytes 2097168 | tf_op jit(solution)/shard_map/psum | solution.py:104
  329.1 1.4 constant_dynamic-slice_fusion
  330.5 225.1 %all-reduce.4.cloned.1.call-done = f32[256,512]{1,0:T(8,128)} async-done(((f32[256,512]{1,0:T(8,128)}), f32[256,512]{1,0:T(8,128)}) %all-reduce.4.cloned.1.call-update) | async-done | bytes 524304 | tf_op jit(solution)/shard_map/psum | solution.py:102
  555.7 1.9 copy.18
  (32 shorter events, 0.3 us)
Async XLA Ops:
  8.0 32.5 %copy-start = (bf16[4096,256]{1,0:T(8,128)(2,1)S(1)}, bf16[4096,256]{1,0:T(8,128)(2,1)}, u32[]{:S(2)}) copy-start(bf16[4096,256]{1,0:T(8,128)(2,1)} %param.12) | copy-start | bytes 6291460
  8.0 118.1 %all-gather.2.cloned.1.call-start = ((), (), s32[]{:S(2)}) async-start(), calls=%async_computation | async-start | bytes 4456448 | tf_op jit(solution)/shard_map/all_gather | solution.py:90
  12.8 4.8 copy-start.3
  12.8 4.8 copy-start.5
  14.5 4.7 copy-start.4
  17.5 4.1 copy-start.2
  17.5 4.1 copy-start.1
  17.5 311.6 %all-reduce.6.cloned.1.call-start = ((), (), s32[]{:S(2)}) async-start(), calls=%async_computation.2 | async-start | bytes 4194304 | tf_op jit(solution)/shard_map/psum | solution.py:104
  21.5 534.1 %all-reduce.4.cloned.1.call-start = ((), (), s32[]{:S(2)}) async-start(), calls=%async_computation.1 | async-start | bytes 1048576 | tf_op jit(solution)/shard_map/psum | solution.py:102
Sparse Core Ops, SparseCore 0:
  17.6 108.4 all-gather.1
Sparse Core Ops, SparseCore 1:
  23.1 306.0 all-reduce.5
  332.7 222.9 all-reduce.3
where the time goes:
time: 565 us
  waiting for transfers between devices  506 us (90%)
  other arithmetic  22.7 us (4%)
  between operations  15.8 us (3%)
  matrix products  14.2 us (3%)
  local copies, waits for them, and re-layouts  6.09 us (1%)
    psum x1, waiting for transfers between devices, body(): grad_one = lax.psum(folded, 'sample')  225 us
    psum x1, waiting for transfers between devices, body(): lax.psum((term_two, term_three), ('sample', 'feat'))  198 us
    all_gather x1, waiting for transfers between devices, body(): piece = lax.all_gather(delta_one, 'feat', axis=0, tiled=True)  82.8 us
    dot_general x1, other arithmetic, body(): jnp.einsum('mij,mjc->mic', tile, features.reshape(group_count, NODES, fea...  17.8 us
    dot_general x5, matrix products, contract_rows(): lax.dot_general(left, right, (((0,), (0,)), ((), ())), preferred_element_...  13.4 us
  transfers between devices with their start and end apart: 3, of which 3 were waited for; matrix products, arithmetic and copies ran while one was open for 6% of the time, Pallas kernels for 0%

commit v1 on v0

--- a/solution.py
+++ b/solution.py
@@ -1,9 +1,13 @@
 import jax
 import jax.numpy as jnp
 from jax import lax
-from jax.sharding import PartitionSpec as P
+from jax.sharding import Mesh, PartitionSpec as P
 
 NODES = 256
+AXES = ("xl", "y", "c", "z", "xh")
+SAMPLE = ("xl", "y", "c")
+FEAT = ("z", "xh")
+Z = 8
 
 
 def count_tiles(neighbor_rows, degrees, width):
@@ -61,6 +65,19 @@
     return (delta_one, term_two, term_three)
 
 
+def turn(block, sign):
+    pairs = []
+    for core in range(2):
+        step = sign if core == 0 else -sign
+        for z in range(Z):
+            pairs.append((core * Z + z, core * Z + (z + step) % Z))
+    return lax.ppermute(block, ("c", "z"), pairs)
+
+
+def swap(block, axis):
+    return lax.ppermute(block, axis, [(0, 1), (1, 0)])
+
+
 def body(
     features,
     pre_one,
@@ -75,6 +92,18 @@
     lists_three,
     degree_three,
 ):
+    bf = jnp.bfloat16
+    f32 = jnp.float32
+    z, xh, c = lax.axis_index("z"), lax.axis_index("xh"), lax.axis_index("c")
+    width = features.shape[1]
+    parts = features.reshape(Z, 2, NODES, width)
+
+    def pick(array, index, axis):
+        return lax.dynamic_index_in_dim(array, index, axis, keepdims=False)
+
+    mine = pick(parts, xh, 1)
+    theirs = swap(pick(parts, 1 - xh, 1), "xh")
+
     delta_one, term_two, term_three = deep_layers(
         pre_one,
         pre_two,
@@ -86,46 +115,76 @@
         lists_three,
         degree_three,
     )
-    feat_width = features.shape[1]
-    piece = lax.all_gather(delta_one, "feat", axis=0, tiled=True)
-    row_count = piece.shape[0]
-    group_count = row_count // NODES
-    tile = count_tiles(lists_one, degree_one, NODES).reshape(group_count, NODES, NODES)
-    summed = jnp.einsum(
-        "mij,mjc->mic",
-        tile,
-        features.reshape(group_count, NODES, feat_width),
-        preferred_element_type=jnp.float32,
-    ).reshape(row_count, feat_width)
-    mean_one = (summed / degree_one.astype(jnp.float32)[:, None]).astype(jnp.bfloat16)
-    folded = contract_rows(mean_one, piece)
-    grad_one = lax.psum(folded, "sample")
-    share = term_two.shape[0] // lax.axis_size("sample")
-    total_two, total_three = lax.psum((term_two, term_three), ("sample", "feat"))
-    offset = lax.axis_index("sample") * share
-    grad_two = lax.dynamic_slice_in_dim(total_two, offset, share, 0)
-    grad_three = lax.dynamic_slice_in_dim(total_three, offset, share, 0)
+    own = z * 2 + xh
+    own_lists = lax.dynamic_slice_in_dim(lists_one, own * NODES, NODES, 0)
+    own_degree = lax.dynamic_slice_in_dim(degree_one, own * NODES, NODES, 0)
+    tile_one = count_tiles(own_lists, own_degree, NODES)
+    scaled = (delta_one.astype(f32) / own_degree.astype(f32)[:, None]).astype(bf)
+    spread = contract_rows(tile_one, scaled).astype(bf)
+
+    blocks = [(spread, z)]
+    ahead = behind = spread
+    sign = 1 - 2 * c
+    for step in range(1, Z // 2 + 1):
+        ahead = turn(ahead, 1)
+        blocks.append((ahead, lax.rem(z - sign * step + Z, Z)))
+        if step < Z // 2:
+            behind = turn(behind, -1)
+            blocks.append((behind, lax.rem(z + sign * step + Z, Z)))
+    part_own = part_other = 0.0
+    for block, index in blocks:
+        part_own = part_own + contract_rows(pick(mine, index, 0), block)
+        part_other = part_other + contract_rows(pick(theirs, index, 0), block)
+
+    terms = jnp.stack([term_two, term_three]).reshape(2, 16, 2, 2, 8, 512)
+    terms = pick(terms, c, 2) + swap(pick(terms, 1 - c, 2).astype(bf), "c").astype(f32)
+    terms = terms.astype(bf).transpose(1, 2, 0, 3, 4)
+
+    first = jnp.where(xh == 0, part_own, part_other)
+    second = jnp.where(xh == 0, part_other, part_own)
+    parted = jnp.stack([first, second]).reshape(2, 2, 128, 512)
+    parted = pick(parted, c, 1) + swap(pick(parted, 1 - c, 1).astype(bf), "c").astype(f32)
+    parted = parted.astype(bf).reshape(2, 16, 1, 8, 512).transpose(1, 0, 2, 3, 4)
+    sent = jnp.concatenate([parted, terms], axis=2).reshape(32, 24, 512)
+    got = lax.all_to_all(sent, ("xl", "y", "xh"), 0, 0)
+    summed = jnp.sum(got.astype(f32), axis=0).astype(bf)
+
+    def spread_out(piece, axes, count):
+        return lax.all_to_all(jnp.broadcast_to(piece[None], (count,) + piece.shape), axes, 0, 0)
+
+    half = spread_out(summed[:8], ("xl", "y"), 16).reshape(128, 512)
+    other = swap(half, "c")
+    low = jnp.where(c == 0, half, other)
+    high = jnp.where(c == 0, other, half)
+    grad_one = jnp.concatenate([low, high], axis=0).astype(f32)
+
+    rest = spread_out(summed[8:], FEAT, 16).reshape(Z, 2, 2, 8, 512)
+    rest = jnp.sum(rest.astype(f32), axis=0)
+    grad_two = rest[:, 0].reshape(16, 512)
+    grad_three = rest[:, 1].reshape(16, 512)
     return (grad_one, grad_two, grad_three)
 
 
 def solution(mesh):
+    fine = Mesh(mesh.devices.reshape(2, 8, 2, 8, 2), AXES)
+    both = SAMPLE + FEAT
     return jax.shard_map(
         body,
-        mesh=mesh,
+        mesh=fine,
         in_specs=(
-            P("sample", "feat"),
-            P(("sample", "feat"), None),
-            P(("sample", "feat"), None),
-            P(("sample", "feat"), None),
+            P(SAMPLE, FEAT),
+            P(both, None),
+            P(both, None),
+            P(both, None),
             P(),
             P(),
-            P("sample", None),
-            P("sample"),
-            P(("sample", "feat"), None),
-            P(("sample", "feat")),
-            P(("sample", "feat"), None),
-            P(("sample", "feat")),
+            P(SAMPLE, None),
+            P(SAMPLE),
+            P(both, None),
+            P(both),
+            P(both, None),
+            P(both),
         ),
-        out_specs=(P("feat", None), P("sample", None), P("sample", None)),
+        out_specs=(P(FEAT, None), P(SAMPLE, None), P(SAMPLE, None)),
         check_vma=False,
     )

time: 565 us -> 153 us (0.27)
  waiting for transfers between devices: 506 us -> 17.4 us
  starting transfers between devices: 0.13 us -> 51.5 us
  blocking collectives: 0 us -> 41.8 us
  between operations: 15.8 us -> 1.18 us
  other arithmetic: 22.7 us -> 8.6 us
  matrix products: 14.2 us -> 25.4 us
    psum x2 -> x0, waiting for transfers between devices: 423 us -> none  [the longest x1 225 us: body(): grad_one = lax.psum(folded, 'sample')]
    all_gather x1 -> x0, waiting for transfers between devices: 82.8 us -> none  [body(): piece = lax.all_gather(delta_one, 'feat', axis=0, tiled=True)]
    ppermute x0 -> x11, starting transfers between devices: none -> 45.7 us  [the longest x7 31.7 us: turn(): return lax.ppermute(block, ('c', 'z'), pairs)]
    all_to_all x0 -> x2, blocking collectives: none -> 41.8 us  [the longest x1 28.5 us: body(): got = lax.all_to_all(sent, ('xl', 'y', 'xh'), 0, 0)]
    dot_general x1 -> x0, other arithmetic: 17.8 us -> none  [body(): jnp.einsum('mij,mjc->mic', tile, features.reshape(group_count, NODES, fea...]
    all_to_all x0 -> x1, waiting for transfers between devices: none -> 12.1 us  [spread_out(): lax.all_to_all(jnp.broadcast_to(piece[None], (count,) + piece.shape), axe...]
    dot_general x5 -> x20, matrix products: 13.4 us -> 24.3 us  [contract_rows(): lax.dot_general(left, right, (((0,), (0,)), ((), ())), preferred_element_...]
    all_to_all x0 -> x1, starting transfers between devices: none -> 5.82 us  [spread_out(): lax.all_to_all(jnp.broadcast_to(piece[None], (count,) + piece.shape), axe...]
  transfers between devices with their start and end apart: 3 -> 12, of which waited for: 3 -> 4; matrix products, arithmetic and copies ran while one was open for 6% -> 16% of each run, Pallas kernels for 0% -> 0%
where the time goes in v1:
time: 153 us; the launch traced here: 151 us
  starting transfers between devices  51.5 us (34%)
  blocking collectives  41.8 us (27%)
  matrix products  25.4 us (17%)
  waiting for transfers between devices  17.4 us (11%)
  other arithmetic  8.6 us (6%)
  local copies, waits for them, and re-layouts  5.6 us (4%)
    ppermute x7, starting transfers between devices, turn(): return lax.ppermute(block, ('c', 'z'), pairs)  31.7 us
    all_to_all x1, blocking collectives, body(): got = lax.all_to_all(sent, ('xl', 'y', 'xh'), 0, 0)  28.5 us
    dot_general x20, matrix products, contract_rows(): lax.dot_general(left, right, (((0,), (0,)), ((), ())), preferred_element_...  24.3 us
    ppermute x4, starting transfers between devices, swap(): return lax.ppermute(block, axis, [(0, 1), (1, 0)])  14 us
    all_to_all x1, blocking collectives, spread_out(): lax.all_to_all(jnp.broadcast_to(piece[None], (count,) + piece.shape), axe...  13.3 us
    all_to_all x1, waiting for transfers between devices, spread_out(): lax.all_to_all(jnp.broadcast_to(piece[None], (count,) + piece.shape), axe...  12.1 us
    all_to_all x1, starting transfers between devices, spread_out(): lax.all_to_all(jnp.broadcast_to(piece[None], (count,) + piece.shape), axe...  5.82 us
    ppermute x7, waiting for transfers between devices, turn(): return lax.ppermute(block, ('c', 'z'), pairs)  5.36 us
  transfers between devices with their start and end apart: 12, of which 4 were waited for; matrix products, arithmetic and copies ran while one was open for 16% of the time, Pallas kernels for 0%

profile of v1, /device:TPU:1, one launch (start us, length us, event | category | flops | bytes accessed | tf_op | source)
XLA Modules:
  0.0 151.4 jit_solution(1162747386383442965)
XLA Ops:
  0.6 0.0 copy-start
  0.7 1.0 broadcast_compare_fusion.23
  1.6 0.7 broadcast_compare_fusion.29
  2.3 0.7 convert_element_type.203
  3.0 0.7 convert_element_type.206
  3.6 0.9 slice_bitcast_fusion.6
  4.5 1.0 fusion.166
  5.5 0.0 copy-start.3
  5.5 1.7 %fusion.7 = bf16[256,512]{1,0:T(8,128)(2,1)S(1)} fusion(bf16[128,512]{1,0:T(8,128)(2,1)} %param.15, bf16[512,512]{1,0:T(8,128)(2,1)} %param.17, bf16[256,512]{1,0:T(8,128)(2,1)} %param.14, f32[128]{0:T(128)S(1)} %convert_element_type.203, s32[128]{0:T(128)S(1)} %get-tuple-element.39, s32[128]{0:T(128)S(1)} %get-tuple-element.40, ...), kind=kOutput, calls=%fused_computation.29 | convolution fusion | flops 102105088 | bytes 1183360 | tf_op jit(solution)/shard_map/dot_general | solution.py:25
  7.3 0.0 copy-start.4
  7.3 1.0 fusion.5
  8.3 1.3 constant_dynamic-slice_fusion
  9.6 4.0 %convolution_convert_fusion = bf16[256,512]{1,0:T(8,128)(2,1)} fusion(bf16[256,512]{1,0:T(8,128)(2,1)} %fusion.5, bf16[256,512]{1,0:T(8,128)(2,1)S(1)} %copy-done.3, f32[256]{0:T(256)S(1)} %convert_element_type.210, s32[256]{0:T(256)S(1)} %bitcast.213, s32[256]{0:T(256)S(1)} %bitcast.200, s32[256]{0:T(256)S(1)} %bitcast.201, s32[256]{0:T(256)S(1)} %bitcast.202, ...), kind=kOutput, calls=%fused_computation.27 | convolution fusion | flops 141688832 | bytes 819456 | tf_op jit(solution)/shard_map/dot_general | solution.py:25
  13.6 11.3 %collective-permute-start = (bf16[256,512]{1,0:T(8,128)(2,1)}, bf16[256,512]{1,0:T(8,128)(2,1)S(1)}, u32[]{:S(2)}, u32[]{:S(2)}) collective-permute-start(bf16[256,512]{1,0:T(8,128)(2,1)} %convolution_convert_fusion), channel_id=1, source_target_pairs={{0,2},{2,4},{4,6},{6,8},{8,10},{10,12},{12,14},{14,0},{16,30},{18,... | collective-permute-start | bytes 786440 | tf_op jit(solution)/shard_map/ppermute | solution.py:74
  24.9 1.9 %collective-permute-start.1 = (bf16[256,512]{1,0:T(8,128)(2,1)}, bf16[256,512]{1,0:T(8,128)(2,1)}, u32[]{:S(2)}, u32[]{:S(2)}) collective-permute-start(bf16[256,512]{1,0:T(8,128)(2,1)} %convolution_convert_fusion), channel_id=1, source_target_pairs={{0,14},{2,0},{4,2},{6,4},{8,6},{10,8},{12,10},{14,12},{16,18},{18,... | collective-permute-start | bytes 786440 | tf_op jit(solution)/shard_map/ppermute | solution.py:74
  26.8 1.1 dynamic-slice_bitcast_fusion
  27.9 4.6 %collective-permute-start.7 = (bf16[8,256,256]{2,1,0:T(8,128)(2,1)}, bf16[8,256,256]{2,1,0:T(8,128)(2,1)}, u32[]{:S(2)}, u32[]{:S(2)}) collective-permute-start(bf16[8,256,256]{2,1,0:T(8,128)(2,1)} %dynamic-slice_bitcast_fusion), channel_id=1, source_target_pairs={{0,1},{1,0},{2,3},{3,2},{4,5},{5,4},{6,7},{7,6},{8,9},{9,8},{10,11... | collective-permute-start | bytes 3145736 | tf_op jit(solution)/shard_map/ppermute | solution.py:78
  32.6 2.2 %fusion.12 = f32[512,512]{1,0:T(8,128)S(1)} fusion(bf16[256,512]{1,0:T(8,128)(2,1)} %copy-done.4, bf16[256,512]{1,0:T(8,128)(2,1)} %param.13, f32[256]{0:T(256)S(1)} %convert_element_type.206, s32[256]{0:T(256)S(1)} %bitcast.196, s32[256]{0:T(256)S(1)} %bitcast.198, s32[256]{0:T(256)S(1)} %bitcast.182, s32[256]{0:T(256)S(1)} %bitcast.184, ...), kind=kOutput, calls=%fused_computation.36 | convolution fusion | flops 204341248 | bytes 1586688 | tf_op jit(solution)/shard_map/dot_general | solution.py:25
  34.8 3.0 %fusion.15 = f32[512,512]{1,0:T(8,128)} fusion(bf16[128,512]{1,0:T(8,128)(2,1)} %param.15, bf16[256,512]{1,0:T(8,128)(2,1)} %param.14, f32[128]{0:T(128)S(1)} %convert_element_type.203, s32[128]{0:T(128)S(1)} %get-tuple-element.39, s32[128]{0:T(128)S(1)} %get-tuple-element.40, s32[128]{0:T(128)S(1)} %get-tuple-element.37, s32[128]{0:T(128)S(1)} %get-tuple-element.38, ...), kind=kOutput, calls=%fused_computation.39 | convolution fusion | flops 101580800 | bytes 1445504 | tf_op jit(solution)/shard_map/dot_general | solution.py:25
  37.8 1.9 %fusion.21 = bf16[2,16,2,8,512]{4,3,0,2,1:T(8,128)(2,1)} fusion(s32[]{:T(128)S(6)} %select_n.130, f32[1,16,2,2,8,512]{5,4,3,2,1,0:T(8,128)S(1)} %bitcast.172, f32[1,16,2,2,8,512]{5,4,3,2,1,0:T(8,128)} %bitcast.174), kind=kLoop, calls=%fused_computation.49 | loop fusion | flops 262144 | bytes 2621444 | tf_op jit(solution)/shard_map/convert_element_type | solution.py:140
  39.7 3.1 %collective-permute-start.9 = (bf16[2,16,2,8,512]{4,3,0,2,1:T(8,128)(2,1)}, bf16[2,16,2,8,512]{4,3,0,2,1:T(8,128)(2,1)}, u32[]{:S(2)}, u32[]{:S(2)}) collective-permute-start(bf16[2,16,2,8,512]{4,3,0,2,1:T(8,128)(2,1)} %fusion.21), channel_id=1, source_target_pairs={{0,16},{16,0},{1,17},{17,1},{2,18},{18,2},{3,19},{19,3},{4,20},{20... | collective-permute-start | bytes 1572872 | tf_op jit(solution)/shard_map/ppermute | solution.py:78
  42.9 1.2 fusion.84
  44.1 0.0 collective-permute-done.1
  44.1 1.9 %collective-permute-start.3 = (bf16[256,512]{1,0:T(8,128)(2,1)}, bf16[256,512]{1,0:T(8,128)(2,1)S(1)}, u32[]{:S(2)}, u32[]{:S(2)}) collective-permute-start(bf16[256,512]{1,0:T(8,128)(2,1)} %collective-permute-done.1), channel_id=1, source_target_pairs={{0,14},{2,0},{4,2},{6,4},{8,6},{10,8},{12,10},{14,12},{16,18},{18,... | collective-permute-start | bytes 786440 | tf_op jit(solution)/shard_map/ppermute | solution.py:74
  46.1 0.0 collective-permute-done
  46.1 4.6 %collective-permute-start.2 = (bf16[256,512]{1,0:T(8,128)(2,1)S(1)}, bf16[256,512]{1,0:T(8,128)(2,1)S(1)}, u32[]{:S(2)}, u32[]{:S(2)}) collective-permute-start(bf16[256,512]{1,0:T(8,128)(2,1)S(1)} %collective-permute-done), channel_id=1, source_target_pairs={{0,2},{2,4},{4,6},{6,8},{8,10},{10,12},{12,14},{14,0},{16,30},{18,... | collective-permute-start | bytes 786440 | tf_op jit(solution)/shard_map/ppermute | solution.py:74
  50.7 0.3 convolution_add_fusion.8
  50.9 1.2 convolution_add_fusion.7
  52.1 0.9 collective-permute-done.3
  53.1 1.9 %collective-permute-start.5 = (bf16[256,512]{1,0:T(8,128)(2,1)S(1)}, bf16[256,512]{1,0:T(8,128)(2,1)S(1)}, u32[]{:S(2)}, u32[]{:S(2)}) collective-permute-start(bf16[256,512]{1,0:T(8,128)(2,1)S(1)} %collective-permute-done.3), channel_id=1, source_target_pairs={{0,14},{2,0},{4,2},{6,4},{8,6},{10,8},{12,10},{14,12},{16,18},{18,... | collective-permute-start | bytes 786440 | tf_op jit(solution)/shard_map/ppermute | solution.py:74
  55.0 0.1 collective-permute-done.2
  55.1 5.0 %collective-permute-start.4 = (bf16[256,512]{1,0:T(8,128)(2,1)S(1)}, bf16[256,512]{1,0:T(8,128)(2,1)S(1)}, u32[]{:S(2)}, u32[]{:S(2)}) collective-permute-start(bf16[256,512]{1,0:T(8,128)(2,1)S(1)} %collective-permute-done.2), channel_id=1, source_target_pairs={{0,2},{2,4},{4,6},{6,8},{8,10},{10,12},{12,14},{14,0},{16,30},{18,... | collective-permute-start | bytes 786440 | tf_op jit(solution)/shard_map/ppermute | solution.py:74
  60.2 0.3 fusion.79
  60.4 0.3 fusion.4
  60.7 4.3 %collective-permute-done.4 = bf16[256,512]{1,0:T(8,128)(2,1)S(1)} collective-permute-done((bf16[256,512]{1,0:T(8,128)(2,1)S(1)}, bf16[256,512]{1,0:T(8,128)(2,1)S(1)}, u32[]{:S(2)}, u32[]{:S(2)}) %collective-permute-start.4) | collective-permute-done | bytes 262176 | tf_op jit(solution)/shard_map/ppermute | solution.py:74
  65.0 5.0 %collective-permute-start.6 = (bf16[256,512]{1,0:T(8,128)(2,1)S(1)}, bf16[256,512]{1,0:T(8,128)(2,1)S(1)}, u32[]{:S(2)}, u32[]{:S(2)}) collective-permute-start(bf16[256,512]{1,0:T(8,128)(2,1)S(1)} %collective-permute-done.4), channel_id=1, source_target_pairs={{0,2},{2,4},{4,6},{6,8},{8,10},{10,12},{12,14},{14,0},{16,30},{18,... | collective-permute-start | bytes 786440 | tf_op jit(solution)/shard_map/ppermute | solution.py:74
  70.0 0.0 collective-permute-done.5
  70.0 0.2 fusion.76
  70.3 0.3 fusion.3
  70.5 0.0 collective-permute-done.7
  70.5 1.3 fusion.70
  71.8 1.2 fusion.72
  73.0 1.1 fusion.67
  74.1 1.2 fusion.64
  75.3 1.3 fusion.2
  76.6 1.2 fusion.1
  77.7 1.2 fusion
  78.9 0.0 collective-permute-done.6
  78.9 1.2 convolution_add_fusion
  80.1 0.3 broadcast_select_fusion.1
  80.4 2.0 %collective-permute-start.8 = (bf16[2,128,512]{2,1,0:T(8,128)(2,1)S(1)}, bf16[2,128,512]{2,1,0:T(8,128)(2,1)}, u32[]{:S(2)}, u32[]{:S(2)}) collective-permute-start(bf16[2,128,512]{2,1,0:T(8,128)(2,1)S(1)} %fusion.30), channel_id=1, source_target_pairs={{0,16},{16,0},{1,17},{17,1},{2,18},{18,2},{3,19},{19,3},{4,20},{20... | collective-permute-start | bytes 786440 | tf_op jit(solution)/shard_map/ppermute | solution.py:78
  82.4 1.5 %fusion.20 = bf16[16,2,2,8,512]{4,3,2,1,0:T(8,128)(2,1)S(1)} fusion(bf16[2,16,2,8,512]{4,3,0,2,1:T(8,128)(2,1)} %collective-permute-done.9, s32[]{:T(128)S(6)} %select_n.129, f32[1,16,2,2,8,512]{5,4,3,2,1,0:T(8,128)} %bitcast.173, f32[1,16,2,2,8,512]{5,4,3,2,1,0:T(8,128)} %bitcast.175), kind=kLoop, calls=%fused_computation.48 | loop fusion | flops 1048576 | bytes 3145732 | tf_op jit(solution)/shard_map/transpose | solution.py:141
  84.0 0.0 collective-permute-done.8
  84.0 1.1 pad_maximum_fusion
  85.1 28.5 %all_to_all.15 = bf16[32,24,512]{2,1,0:T(8,128)(2,1)S(1)} all-to-all(bf16[32,24,512]{2,1,0:T(8,128)(2,1)S(1)} %bitcast.176), channel_id=1, replica_groups=mesh['xl'=2,'y'=8,'c'=2,'z'=8,'xh'=2] {'xl','y','xh'}, dimensions={0} | all-to-all | bytes 1572864 | tf_op jit(solution)/shard_map/all_to_all | solution.py:149
  113.6 0.1 reduce_sum.21
  113.7 13.3 %all_to_all.16 = bf16[16,8,512]{2,1,0:T(8,128)(2,1)S(1)} all-to-all(bf16[16,8,512]{2,1,0:T(8,128)(2,1)S(1)} %broadcast_in_dim.9), channel_id=1, replica_groups=mesh['xl'=2,'y'=8,'c'=2,'z'=8,'xh'=2] {'xl','y'}, dimensions={0} | all-to-all | bytes 262144 | tf_op jit(solution)/shard_map/all_to_all | solution.py:153
  127.0 4.2 %collective-permute-start.10 = (bf16[128,512]{1,0:T(8,128)(2,1)S(1)}, bf16[128,512]{1,0:T(8,128)(2,1)S(1)}, u32[]{:S(2)}, u32[]{:S(2)}) collective-permute-start(bf16[128,512]{1,0:T(8,128)(2,1)S(1)} %bitcast.178), channel_id=1, source_target_pairs={{0,16},{16,0},{1,17},{17,1},{2,18},{18,2},{3,19},{19,3},{4,20},{20... | collective-permute-start | bytes 393224 | tf_op jit(solution)/shard_map/ppermute | solution.py:78
  131.3 0.7 broadcast_in_dim.10
  132.0 5.8 %all-to-all-start.2 = ((bf16[16,16,512]{2,1,0:T(8,128)(2,1)}), bf16[16,16,512]{2,1,0:T(8,128)(2,1)S(1)}, u32[]{:S(2)}, u32[]{:S(2)}) async-start(bf16[16,16,512]{2,1,0:T(8,128)(2,1)} %broadcast_in_dim.10), calls=%async_computation.2 | async-start | bytes 524288 | tf_op jit(solution)/shard_map/all_to_all | solution.py:153
  137.8 0.0 collective-permute-done.10
  137.8 0.9 maximum_convert_fusion
  138.7 12.1 %all-to-all-done.2 = bf16[16,16,512]{2,1,0:T(8,128)(2,1)S(1)} async-done(((bf16[16,16,512]{2,1,0:T(8,128)(2,1)}), bf16[16,16,512]{2,1,0:T(8,128)(2,1)S(1)}, u32[]{:S(2)}, u32[]{:S(2)}) %all-to-all-start.2) | async-done | bytes 262176 | tf_op jit(solution)/shard_map/all_to_all | solution.py:153
  150.8 0.6 slice_bitcast_fusion
  (16 shorter events, 0.1 us)
Async XLA Ops:
  0.6 26.2 %copy-start = (bf16[4096,256]{1,0:T(8,128)(2,1)S(1)}, bf16[4096,256]{1,0:T(8,128)(2,1)}, u32[]{:S(2)}) copy-start(bf16[4096,256]{1,0:T(8,128)(2,1)} %param.12) | copy-start | bytes 6291460
  0.6 6.6 %copy-start.2 = (bf16[512,512]{1,0:T(8,128)(2,1)S(1)}, bf16[512,512]{1,0:T(8,128)(2,1)}, u32[]{:S(2)}) copy-start(bf16[512,512]{1,0:T(8,128)(2,1)} %param.16) | copy-start | bytes 1572868
  5.5 4.1 %copy-start.3 = (bf16[256,512]{1,0:T(8,128)(2,1)S(1)}, bf16[256,512]{1,0:T(8,128)(2,1)}, u32[]{:S(2)}) copy-start(bf16[256,512]{1,0:T(8,128)(2,1)} %param.13) | copy-start | bytes 786436
  7.3 6.3 %copy-start.4 = (bf16[256,512]{1,0:T(8,128)(2,1)}, bf16[256,512]{1,0:T(8,128)(2,1)S(1)}, u32[]{:S(2)}) copy-start(bf16[256,512]{1,0:T(8,128)(2,1)S(1)} %fusion.7) | copy-start | bytes 786436
  13.6 32.5 %collective-permute-start = (bf16[256,512]{1,0:T(8,128)(2,1)}, bf16[256,512]{1,0:T(8,128)(2,1)S(1)}, u32[]{:S(2)}, u32[]{:S(2)}) collective-permute-start(bf16[256,512]{1,0:T(8,128)(2,1)} %convolution_convert_fusion), channel_id=1, source_target_pairs={{0,2},{2,4},{4,6},{6,8},{8,10},{10,12},{12,14},{14,0},{16,30},{18,... | collective-permute-start | bytes 786440 | tf_op jit(solution)/shard_map/ppermute | solution.py:74
  24.9 19.2 %collective-permute-start.1 = (bf16[256,512]{1,0:T(8,128)(2,1)}, bf16[256,512]{1,0:T(8,128)(2,1)}, u32[]{:S(2)}, u32[]{:S(2)}) collective-permute-start(bf16[256,512]{1,0:T(8,128)(2,1)} %convolution_convert_fusion), channel_id=1, source_target_pairs={{0,14},{2,0},{4,2},{6,4},{8,6},{10,8},{12,10},{14,12},{16,18},{18,... | collective-permute-start | bytes 786440 | tf_op jit(solution)/shard_map/ppermute | solution.py:74
  27.9 42.6 %collective-permute-start.7 = (bf16[8,256,256]{2,1,0:T(8,128)(2,1)}, bf16[8,256,256]{2,1,0:T(8,128)(2,1)}, u32[]{:S(2)}, u32[]{:S(2)}) collective-permute-start(bf16[8,256,256]{2,1,0:T(8,128)(2,1)} %dynamic-slice_bitcast_fusion), channel_id=1, source_target_pairs={{0,1},{1,0},{2,3},{3,2},{4,5},{5,4},{6,7},{7,6},{8,9},{9,8},{10,11... | collective-permute-start | bytes 3145736 | tf_op jit(solution)/shard_map/ppermute | solution.py:78
  34.8 4.9 %copy-start.1 = (f32[512,512]{1,0:T(8,128)}, f32[512,512]{1,0:T(8,128)S(1)}, u32[]{:S(2)}) copy-start(f32[512,512]{1,0:T(8,128)S(1)} %fusion.12) | copy-start | bytes 3145732
  39.7 42.7 %collective-permute-start.9 = (bf16[2,16,2,8,512]{4,3,0,2,1:T(8,128)(2,1)}, bf16[2,16,2,8,512]{4,3,0,2,1:T(8,128)(2,1)}, u32[]{:S(2)}, u32[]{:S(2)}) collective-permute-start(bf16[2,16,2,8,512]{4,3,0,2,1:T(8,128)(2,1)} %fusion.21), channel_id=1, source_target_pairs={{0,16},{16,0},{1,17},{17,1},{2,18},{18,2},{3,19},{19,3},{4,20},{20... | collective-permute-start | bytes 1572872 | tf_op jit(solution)/shard_map/ppermute | solution.py:78
  44.1 8.9 %collective-permute-start.3 = (bf16[256,512]{1,0:T(8,128)(2,1)}, bf16[256,512]{1,0:T(8,128)(2,1)S(1)}, u32[]{:S(2)}, u32[]{:S(2)}) collective-permute-start(bf16[256,512]{1,0:T(8,128)(2,1)} %collective-permute-done.1), channel_id=1, source_target_pairs={{0,14},{2,0},{4,2},{6,4},{8,6},{10,8},{12,10},{14,12},{16,18},{18,... | collective-permute-start | bytes 786440 | tf_op jit(solution)/shard_map/ppermute | solution.py:74
  46.1 9.1 %collective-permute-start.2 = (bf16[256,512]{1,0:T(8,128)(2,1)S(1)}, bf16[256,512]{1,0:T(8,128)(2,1)S(1)}, u32[]{:S(2)}, u32[]{:S(2)}) collective-permute-start(bf16[256,512]{1,0:T(8,128)(2,1)S(1)} %collective-permute-done), channel_id=1, source_target_pairs={{0,2},{2,4},{4,6},{6,8},{8,10},{10,12},{12,14},{14,0},{16,30},{18,... | collective-permute-start | bytes 786440 | tf_op jit(solution)/shard_map/ppermute | solution.py:74
  53.1 16.9 %collective-permute-start.5 = (bf16[256,512]{1,0:T(8,128)(2,1)S(1)}, bf16[256,512]{1,0:T(8,128)(2,1)S(1)}, u32[]{:S(2)}, u32[]{:S(2)}) collective-permute-start(bf16[256,512]{1,0:T(8,128)(2,1)S(1)} %collective-permute-done.3), channel_id=1, source_target_pairs={{0,14},{2,0},{4,2},{6,4},{8,6},{10,8},{12,10},{14,12},{16,18},{18,... | collective-permute-start | bytes 786440 | tf_op jit(solution)/shard_map/ppermute | solution.py:74
  55.1 9.8 %collective-permute-start.4 = (bf16[256,512]{1,0:T(8,128)(2,1)S(1)}, bf16[256,512]{1,0:T(8,128)(2,1)S(1)}, u32[]{:S(2)}, u32[]{:S(2)}) collective-permute-start(bf16[256,512]{1,0:T(8,128)(2,1)S(1)} %collective-permute-done.2), channel_id=1, source_target_pairs={{0,2},{2,4},{4,6},{6,8},{8,10},{10,12},{12,14},{14,0},{16,30},{18,... | collective-permute-start | bytes 786440 | tf_op jit(solution)/shard_map/ppermute | solution.py:74
  65.0 13.9 %collective-permute-start.6 = (bf16[256,512]{1,0:T(8,128)(2,1)S(1)}, bf16[256,512]{1,0:T(8,128)(2,1)S(1)}, u32[]{:S(2)}, u32[]{:S(2)}) collective-permute-start(bf16[256,512]{1,0:T(8,128)(2,1)S(1)} %collective-permute-done.4), channel_id=1, source_target_pairs={{0,2},{2,4},{4,6},{6,8},{8,10},{10,12},{12,14},{14,0},{16,30},{18,... | collective-permute-start | bytes 786440 | tf_op jit(solution)/shard_map/ppermute | solution.py:74
  80.4 3.6 %collective-permute-start.8 = (bf16[2,128,512]{2,1,0:T(8,128)(2,1)S(1)}, bf16[2,128,512]{2,1,0:T(8,128)(2,1)}, u32[]{:S(2)}, u32[]{:S(2)}) collective-permute-start(bf16[2,128,512]{2,1,0:T(8,128)(2,1)S(1)} %fusion.30), channel_id=1, source_target_pairs={{0,16},{16,0},{1,17},{17,1},{2,18},{18,2},{3,19},{19,3},{4,20},{20... | collective-permute-start | bytes 786440 | tf_op jit(solution)/shard_map/ppermute | solution.py:78
  127.0 10.8 %collective-permute-start.10 = (bf16[128,512]{1,0:T(8,128)(2,1)S(1)}, bf16[128,512]{1,0:T(8,128)(2,1)S(1)}, u32[]{:S(2)}, u32[]{:S(2)}) collective-permute-start(bf16[128,512]{1,0:T(8,128)(2,1)S(1)} %bitcast.178), channel_id=1, source_target_pairs={{0,16},{16,0},{1,17},{17,1},{2,18},{18,2},{3,19},{19,3},{4,20},{20... | collective-permute-start | bytes 393224 | tf_op jit(solution)/shard_map/ppermute | solution.py:78
  132.0 18.8 %all-to-all-start.2 = ((bf16[16,16,512]{2,1,0:T(8,128)(2,1)}), bf16[16,16,512]{2,1,0:T(8,128)(2,1)S(1)}, u32[]{:S(2)}, u32[]{:S(2)}) async-start(bf16[16,16,512]{2,1,0:T(8,128)(2,1)} %broadcast_in_dim.10), calls=%async_computation.2 | async-start | bytes 524288 | tf_op jit(solution)/shard_map/all_to_all | solution.py:153

commit v2 on v1

v2 whole, which is shorter than its diff:
```python
import jax
import jax.numpy as jnp
from jax import lax
from jax.experimental import pallas as pl
from jax.experimental.pallas import tpu as pltpu
from jax.sharding import Mesh, PartitionSpec as P

NODES = 256
TGT = 128
HIDDEN = 512
AXES = ("xl", "y", "c", "z", "xh")
SAMPLE = ("xl", "y", "c")
FEAT = ("z", "xh")
Z = 8
BF = jnp.bfloat16
F32 = jnp.float32
MIB = 1024 * 1024


def mul(left, right, left_dim, right_dim):
    return lax.dot_general(
        left,
        right,
        (((left_dim,), (right_dim,)), ((), ())),
        preferred_element_type=F32,
    )


def tile_t(lists, degree):
    fan, rows = lists.shape
    nodes = lax.broadcasted_iota(jnp.int32, (NODES, rows), 0)
    total = jnp.zeros((NODES, rows), F32)
    for k in range(fan):
        valid = jnp.where(k < degree, lists[k : k + 1, :], -1)
        total = total + jnp.where(nodes == valid, 1.0, 0.0)
    return total.astype(BF)


def inverse_column(degree):
    rows = degree.shape[1]
    line = lax.broadcasted_iota(jnp.int32, (rows, rows), 0)
    column = lax.broadcasted_iota(jnp.int32, (rows, rows), 1)
    eye = jnp.where(line == column, 1.0, 0.0).astype(BF)
    spread = jnp.broadcast_to(degree.astype(F32), (128, rows)).astype(BF)
    return 1.0 / mul(eye, spread, 1, 1)


def scale_rows(values, inverse):
    return values * jnp.concatenate([inverse] * (values.shape[1] // 128), axis=1)


IN_VMEM = pl.BlockSpec(memory_space=pltpu.VMEM)
IN_HBM = pl.BlockSpec(memory_space=pltpu.HBM)
IN_SMEM = pl.BlockSpec(memory_space=pltpu.SMEM)


def call(kernel, name, out_shape, in_specs, scratch, flops, limit, operands):
    return pl.pallas_call(
        kernel,
        out_shape=out_shape,
        in_specs=in_specs,
        out_specs=tuple(IN_VMEM for unused in out_shape),
        scratch_shapes=scratch,
        compiler_params=pltpu.CompilerParams(vmem_limit_bytes=limit * MIB),
        cost_estimate=pl.CostEstimate(
            flops=flops, bytes_accessed=3_000_000, transcendentals=0
        ),
        name=name,
    )(*operands)


def chain_kernel(
    own,
    weight_three_hbm,
    cotangent_hbm,
    lists_three_hbm,
    degree_three_hbm,
    pre_two_hbm,
    lists_two_hbm,
    degree_two_hbm,
    weight_two_hbm,
    lists_one_hbm,
    degree_one_hbm,
    pre_one_hbm,
    spread_out,
    delta_out,
    tile_two_out,
    tile_three_out,
    weight_three,
    cotangent,
    lists_three,
    degree_three,
    pre_two,
    lists_two,
    degree_two,
    weight_two,
    lists_one,
    degree_one,
    pre_one,
    sems,
):
    columns = pl.ds(pl.multiple_of(own[0] * NODES, NODES), NODES)
    pairs = [
        (lists_three_hbm, lists_three),
        (degree_three_hbm, degree_three),
        (cotangent_hbm, cotangent),
        (weight_three_hbm, weight_three),
        (lists_two_hbm, lists_two),
        (degree_two_hbm, degree_two),
        (lists_one_hbm.at[:, columns], lists_one),
        (degree_one_hbm.at[:, columns], degree_one),
        (pre_two_hbm, pre_two),
        (weight_two_hbm, weight_two),
        (pre_one_hbm, pre_one),
    ]
    copies = [
        pltpu.make_async_copy(source, target, sems.at[index])
        for index, (source, target) in enumerate(pairs)
    ]
    for copy in copies:
        copy.start()
    for copy in copies[:2]:
        copy.wait()
    tile_three = tile_t(lists_three[...], degree_three[...])
    inverse_three = inverse_column(degree_three[...])
    tile_three_out[...] = tile_three
    for copy in copies[2:4]:
        copy.wait()
    back_three = scale_rows(mul(cotangent[...], weight_three[...], 1, 1), inverse_three)
    for copy in copies[4:8]:
        copy.wait()
    tile_two = tile_t(lists_two[...], degree_two[...])
    inverse_two = inverse_column(degree_two[...])
    tile_two_out[...] = tile_two
    tile_one = tile_t(lists_one[...], degree_one[...])
    inverse_one = inverse_column(degree_one[...])
    for copy in copies[8:]:
        copy.wait()
    up_two = mul(tile_three, back_three.astype(BF), 1, 0)
    delta_two = jnp.where(pre_two[...].astype(F32) > 0, up_two, 0.0).astype(BF)
    delta_out[...] = delta_two
    back_two = scale_rows(mul(delta_two, weight_two[...], 1, 1), inverse_two)
    up_one = mul(tile_two, back_two.astype(BF), 1, 0)
    delta_one = jnp.where(pre_one[...].astype(F32) > 0, up_one, 0.0).astype(BF)
    scaled = scale_rows(delta_one.astype(F32), inverse_one)
    high = scaled.astype(BF)
    low = (scaled - high.astype(F32)).astype(BF)
    spread = mul(tile_one, high, 1, 0) + mul(tile_one, low, 1, 0)
    spread_out[...] = spread.astype(BF)


def run_chain(own, arrays):
    shapes = [(array.shape, array.dtype) for array in arrays]
    for index in (8, 9):
        shapes[index] = ((shapes[index][0][0], NODES), shapes[index][1])
    return call(
        chain_kernel,
        "chain",
        (
            jax.ShapeDtypeStruct((NODES, HIDDEN), BF),
            jax.ShapeDtypeStruct((NODES, HIDDEN), BF),
            jax.ShapeDtypeStruct((NODES, NODES), BF),
            jax.ShapeDtypeStruct((NODES, TGT), BF),
        ),
        [IN_SMEM] + [IN_HBM] * len(arrays),
        [pltpu.VMEM(shape, kind) for shape, kind in shapes]
        + [pltpu.SemaphoreType.DMA((len(arrays),))],
        2 * 218_000_000,
        24,
        [own] + arrays,
    )


def terms_kernel(
    core,
    pre_one_hbm,
    pre_two_hbm,
    cotangent_hbm,
    degree_two_hbm,
    degree_three_hbm,
    delta_two,
    tile_two,
    tile_three,
    sent,
    kept,
    pre_one,
    pre_two,
    cotangent,
    degree_two,
    degree_three,
    total,
    sems,
):
    pairs = [
        (degree_three_hbm, degree_three),
        (pre_two_hbm, pre_two),
        (cotangent_hbm, cotangent),
        (degree_two_hbm, degree_two),
        (pre_one_hbm, pre_one),
    ]
    copies = [
        pltpu.make_async_copy(source, target, sems.at[index])
        for index, (source, target) in enumerate(pairs)
    ]
    for copy in copies:
        copy.start()
    for copy in copies:
        copy.wait()
    hidden_two = jnp.maximum(pre_two[...].astype(F32), 0.0).astype(BF)
    hidden_one = jnp.maximum(pre_one[...].astype(F32), 0.0).astype(BF)
    mean_three = scale_rows(
        mul(tile_three[...], hidden_two, 0, 0), inverse_column(degree_three[...])
    ).astype(BF)
    mean_two = scale_rows(
        mul(tile_two[...], hidden_one, 0, 0), inverse_column(degree_two[...])
    ).astype(BF)
    here = core[0]
    for which, (left, right) in enumerate(
        [(mean_two, delta_two[...]), (mean_three, cotangent[...])]
    ):
        total[...] = mul(left, right, 0, 0)
        for piece in range(16):
            mine = pl.multiple_of(piece * 32 + here * 16, 16)
            other = pl.multiple_of(piece * 32 + (1 - here) * 16, 16)
            kept[piece, which] = total[pl.ds(mine, 16), :]
            sent[piece, which] = total[pl.ds(other, 16), :].astype(BF)


def run_terms(core, inputs, inner):
    return call(
        terms_kernel,
        "terms",
        (
            jax.ShapeDtypeStruct((16, 2, 16, HIDDEN), BF),
            jax.ShapeDtypeStruct((16, 2, 16, HIDDEN), F32),
        ),
        [IN_SMEM] + [IN_HBM] * len(inputs) + [IN_VMEM] * len(inner),
        [pltpu.VMEM(array.shape, array.dtype) for array in inputs]
        + [
            pltpu.VMEM((HIDDEN, HIDDEN), F32),
            pltpu.SemaphoreType.DMA((len(inputs),)),
        ],
        2 * 151_000_000,
        24,
        [core] + inputs + inner,
    )


def run_fold(features, theirs, blocks, own_rows, other_rows, before):
    count, given = len(own_rows), len(blocks)
    width = features.shape[1]
    where = jnp.stack(list(own_rows) + list(other_rows)).astype(jnp.int32)
    start = [] if before is None else [before]
    extra = count > given

    def kernel(where, features_hbm, theirs_hbm, *refs):
        blocks, refs = refs[:given], refs[given:]
        start, refs = refs[: len(before_list)], refs[len(before_list) :]
        total, refs = refs[0], refs[1:]
        if extra:
            last, refs = refs[0], refs[1:]
        parts, sems = refs
        copies = []
        for side, source in enumerate((features_hbm, theirs_hbm)):
            for index in range(count):
                row = pl.multiple_of(where[side * count + index] * NODES, NODES)
                copy = pltpu.make_async_copy(
                    source.at[pl.ds(row, NODES), :],
                    parts.at[side, pl.ds(index * NODES, NODES), :],
                    sems.at[side, index],
                )
                copy.start()
                copies.append(copy)
        stacked = jnp.concatenate([block[...] for block in blocks], axis=0)
        for side in range(2):
            for copy in copies[side * count : side * count + given]:
                copy.wait()
            term = mul(parts[side, : given * NODES, :], stacked, 0, 0)
            total[side] = start[0][side] + term if start else term
        if extra:
            for side in range(2):
                copies[side * count + given].wait()
                last[side] = parts[side, given * NODES :, :].T

    before_list = start
    out_shape = (jax.ShapeDtypeStruct((2, width, HIDDEN), F32),)
    if extra:
        out_shape += (jax.ShapeDtypeStruct((2, width, NODES), BF),)
    return call(
        kernel,
        "fold",
        out_shape,
        [IN_SMEM, IN_HBM, IN_HBM] + [IN_VMEM] * (given + len(start)),
        [
            pltpu.VMEM((2, count * NODES, width), BF),
            pltpu.SemaphoreType.DMA((2, count)),
        ],
        given * 2 * 67_000_000,
        24,
        [where, features, theirs] + blocks + start,
    )


def run_last(total, last, block, core, half):
    width = total.shape[1]
    rows = width // 2
    where = jnp.stack([core, half]).astype(jnp.int32)

    def kernel(where, total, last, block, sent, kept, scratch):
        core, half = where[0], where[1]
        keep = pl.multiple_of(core * rows, rows)
        send = pl.multiple_of((1 - core) * rows, rows)
        for side in range(2):
            scratch[...] = total[side] + mul(last[side], block[...], 1, 0)
            place = half if side == 0 else 1 - half
            kept[place] = scratch[pl.ds(keep, rows), :]
            sent[place] = scratch[pl.ds(send, rows), :].astype(BF)

    return call(
        kernel,
        "last",
        (
            jax.ShapeDtypeStruct((2, rows, HIDDEN), BF),
            jax.ShapeDtypeStruct((2, rows, HIDDEN), F32),
        ),
        [IN_SMEM] + [IN_VMEM] * 3,
        [pltpu.VMEM((width, HIDDEN), F32)],
        2 * 70_000_000,
        16,
        [where, total, last, block],
    )


def turn(block, sign):
    pairs = []
    for core in range(2):
        step = sign if core == 0 else -sign
        for z in range(Z):
            pairs.append((core * Z + z, core * Z + (z + step) % Z))
    return lax.ppermute(block, ("c", "z"), pairs)


def swap(block, axis):
    return lax.ppermute(block, axis, [(0, 1), (1, 0)])


def after(*values):
    return lax.optimization_barrier(values)


def spread_out(piece, axes, count):
    return lax.all_to_all(jnp.broadcast_to(piece[None], (count,) + piece.shape), axes, 0, 0)


def body(
    features,
    pre_one,
    pre_two,
    cotangent,
    weight_two,
    weight_three,
    lists_one,
    degree_one,
    lists_two,
    degree_two,
    lists_three,
    degree_three,
):
    z, xh, c = lax.axis_index("z"), lax.axis_index("xh"), lax.axis_index("c")
    width = features.shape[1]

    own = jnp.reshape(z * 2 + xh, (1,)).astype(jnp.int32)
    core = jnp.reshape(c, (1,)).astype(jnp.int32)

    parts = features.reshape(Z, 2, NODES, width)
    give = lax.dynamic_index_in_dim(parts, 1 - xh, 1, keepdims=False)
    own, give = after(own, give)
    theirs = swap(give, "xh").reshape(Z * NODES, width)

    lists = [lists_one.T, lists_two.T, lists_three.T]
    degrees = [degree_one[None], degree_two[None], degree_three[None]]
    spread, delta_two, tile_two, tile_three = run_chain(
        own,
        [weight_three, cotangent, lists[2], degrees[2], pre_two, lists[1], degrees[1]]
        + [weight_two, lists[0], degrees[0], pre_one],
    )

    ahead, behind = [spread], [spread]

    def step_on():
        ahead.append(turn(ahead[-1], 1))
        if len(behind) < Z // 2:
            behind.append(turn(behind[-1], -1))

    step_on()
    sent, kept = run_terms(
        core,
        [pre_one, pre_two, cotangent, degrees[1], degrees[2]],
        [delta_two, tile_two, tile_three],
    )
    ahead[1], behind[1], sent = after(ahead[1], behind[1], sent)
    step_on()
    other = swap(sent, "c")
    ahead[2], behind[2], other = after(ahead[2], behind[2], other)
    step_on()
    terms = (kept + other.astype(F32)).astype(BF).reshape(32, 16, HIDDEN)
    terms = lax.all_to_all(terms, ("xl", "y", "xh"), 0, 0)
    ahead[3], behind[3] = after(ahead[3], behind[3])
    step_on()

    sign = 1 - 2 * c

    def places(steps):
        rows = [lax.rem(z + sign * step + Z, Z) for step in steps]
        return [row * 2 + xh for row in rows], rows

    (total,) = run_fold(
        features, theirs, [spread, behind[1], ahead[1], behind[2], ahead[2]],
        *places([0, 1, -1, 2, -2]), None
    )
    total, last = run_fold(
        features, theirs, [behind[3], ahead[3]], *places([3, -3, -4]), total
    )
    sent, kept = run_last(total, last, ahead[4], c, xh)
    total = (kept + swap(sent, "c").astype(F32)).astype(BF).reshape(32, 8, HIDDEN)
    total = lax.all_to_all(total, ("xh", "xl", "y"), 0, 0)

    def double(terms, step):
        return terms + lax.ppermute(terms, "z", [(k, k ^ step) for k in range(Z)])

    terms = jnp.sum(terms.astype(F32), axis=0)
    terms = double(double(terms, 1), 2)
    total, terms = after(total, terms)
    total = jnp.sum(total.astype(F32), axis=0).astype(BF)
    total = spread_out(total, ("xl", "y"), 16).reshape(width // 2, HIDDEN)
    terms = double(terms, 4)
    other = swap(terms, "xh")
    total, terms, other = after(total, terms, other)
    grad_one = lax.all_gather(total, "c", axis=0, tiled=True).astype(F32)
    grad_two = jnp.where(xh == 0, terms, other)
    grad_three = jnp.where(xh == 0, other, terms)
    return (grad_one, grad_two, grad_three)


def solution(mesh):
    fine = Mesh(mesh.devices.reshape(2, 8, 2, 8, 2), AXES)
    both = SAMPLE + FEAT
    return jax.shard_map(
        body,
        mesh=fine,
        in_specs=(
            P(SAMPLE, FEAT),
            P(both, None),
            P(both, None),
            P(both, None),
            P(),
            P(),
            P(SAMPLE, None),
            P(SAMPLE),
            P(both, None),
            P(both),
            P(both, None),
            P(both),
        ),
        out_specs=(P(FEAT, None), P(SAMPLE, None), P(SAMPLE, None)),
        check_vma=False,
    )
```

time: 153 us -> 132 us (0.86)
  blocking collectives: 41.8 us -> 7.14 us
  matrix products: 25.4 us -> 0 us
  starting transfers between devices: 51.5 us -> 75.3 us
  Pallas kernels: 0 us -> 13.1 us
  waiting for transfers between devices: 17.4 us -> 23.6 us
  other arithmetic: 8.6 us -> 4.5 us
    all_to_all x2 -> x0, blocking collectives: 41.8 us -> none  [the longest x1 28.5 us: body(): got = lax.all_to_all(sent, ('xl', 'y', 'xh'), 0, 0)]
    dot_general x21 -> x0, matrix products: 25.4 us -> none  [the longest x20 24.3 us: contract_rows(): lax.dot_general(left, right, (((0,), (0,)), ((), ())), preferred_element_...]
    all_to_all x0 -> x2, starting transfers between devices: none -> 17.3 us  [the longest x1 9.42 us: body(): total = lax.all_to_all(total, ('xh', 'xl', 'y'), 0, 0)]
    pallas_call x0 -> x5, Pallas kernels: none -> 13.1 us  [call(): pl.pallas_call(kernel, out_shape=out_shape, in_specs=in_specs, out_specs=...]
    all_to_all x1, waiting for transfers between devices: 12.1 us -> 0.01 us  [spread_out(): lax.all_to_all(jnp.broadcast_to(piece[None], (count,) + piece.shape), axe...]
    ppermute x0 -> x3, waiting for transfers between devices: none -> 9.85 us  [double(): return terms + lax.ppermute(terms, 'z', [(k, k ^ step) for k in range(Z)])]
    ppermute x0 -> x3, starting transfers between devices: none -> 9.74 us  [double(): return terms + lax.ppermute(terms, 'z', [(k, k ^ step) for k in range(Z)])]
    all_gather x0 -> x1, blocking collectives: none -> 7.14 us  [body(): grad_one = lax.all_gather(total, 'c', axis=0, tiled=True).astype(F32)]
  transfers between devices with their start and end apart: 12 -> 17, of which waited for: 4 -> 8; matrix products, arithmetic and copies ran while one was open for 16% -> 2% of each run, Pallas kernels for 0% -> 7%
where the time goes in v2:
time: 132 us; the launch traced here: 131 us
  starting transfers between devices  75.3 us (57%)
  waiting for transfers between devices  23.6 us (18%)
  Pallas kernels  13.1 us (10%)
  blocking collectives  7.14 us (5%)
  local copies, waits for them, and re-layouts  6.31 us (5%)
  other arithmetic  4.5 us (3%)
    ppermute x7, starting transfers between devices, turn(): return lax.ppermute(block, ('c', 'z'), pairs)  27.7 us
    ppermute x4, starting transfers between devices, swap(): return lax.ppermute(block, axis, [(0, 1), (1, 0)])  13.4 us
    pallas_call x5, Pallas kernels, call(): pl.pallas_call(kernel, out_shape=out_shape, in_specs=in_specs, out_specs=...  13.1 us
    ppermute x7, waiting for transfers between devices, turn(): return lax.ppermute(block, ('c', 'z'), pairs)  10.8 us
    ppermute x3, waiting for transfers between devices, double(): return terms + lax.ppermute(terms, 'z', [(k, k ^ step) for k in range(Z)])  9.85 us
    ppermute x3, starting transfers between devices, double(): return terms + lax.ppermute(terms, 'z', [(k, k ^ step) for k in range(Z)])  9.74 us
    all_to_all x1, starting transfers between devices, body(): total = lax.all_to_all(total, ('xh', 'xl', 'y'), 0, 0)  9.42 us
    all_to_all x1, starting transfers between devices, body(): terms = lax.all_to_all(terms, ('xl', 'y', 'xh'), 0, 0)  7.92 us
  transfers between devices with their start and end apart: 17, of which 8 were waited for; matrix products, arithmetic and copies ran while one was open for 2% of the time, Pallas kernels for 7%

profile of v2, /device:TPU:1, one launch (start us, length us, event | category | flops | bytes accessed | tf_op | source)
XLA Modules:
  0.0 131.0 jit_solution(17911937437154975775)
XLA Ops:
  0.6 0.0 copy-start.11
  0.6 0.0 copy-start.10
  0.7 0.0 copy-start.9
  0.7 0.0 copy-start.7
  0.7 0.0 copy-start.3
  0.7 0.0 copy-start.8
  0.7 0.0 copy-start.5
  0.8 2.4 %dynamic-slice_bitcast_fusion = bf16[8,256,256]{2,1,0:T(8,128)(2,1)} fusion(bf16[8,2,256,256]{3,2,1,0:T(8,128)(2,1)} %bitcast.32, s32[]{:T(128)S(6)} %select_n.16), kind=kLoop, calls=%fused_computation.2 | loop fusion | bytes 2097156 | tf_op jit(solution)/shard_map/jit(dynamic_index_in_dim)/squeeze | solution.py:376
  3.3 3.5 %chain.1 = (bf16[256,512]{1,0:T(8,128)(2,1)S(1)}, bf16[256,512]{1,0:T(8,128)(2,1)S(1)}, bf16[256,256]{1,0:T(8,128)(2,1)S(1)}, bf16[256,128]{1,0:T(8,128)(2,1)S(1)}) custom-call(s32[1]{0:T(128)} %bitcast.8.own, bf16[512,512]{1,0:T(8,128)(2,1)S(1)} %copy-done.1, bf16[128,512]{1,0:T(8,128)(2,1)S(1)} %copy-done.6, s32[5,128]{1,0:T(8,128)S(1)} %bitcast.38, ...), custom_call_target="tpu_custom_call" | custom-call | flops 436000000 | bytes 3000000 | tf_op jit(solution)/shard_map/chain/pallas_call | solution.py:58
  6.7 0.0 copy-start.12
  6.8 0.6 copy-done.12
  7.4 0.6 copy-done.14
  8.0 11.5 %collective-permute-start.1 = (bf16[256,512]{1,0:T(8,128)(2,1)S(1)}, bf16[256,512]{1,0:T(8,128)(2,1)}, u32[]{:S(2)}, u32[]{:S(2)}) collective-permute-start(bf16[256,512]{1,0:T(8,128)(2,1)S(1)} %get-tuple-element.30.refs_0_), channel_id=1, source_target_pairs={{0,2},{2,4},{4,6},{6,8},{8,10},{10,12},{12,14},{14,0},{16,30},{18,... | collective-permute-start | bytes 786440 | tf_op jit(solution)/shard_map/ppermute | solution.py:340
  19.5 1.9 %collective-permute-start.2 = (bf16[256,512]{1,0:T(8,128)(2,1)S(1)}, bf16[256,512]{1,0:T(8,128)(2,1)}, u32[]{:S(2)}, u32[]{:S(2)}) collective-permute-start(bf16[256,512]{1,0:T(8,128)(2,1)S(1)} %get-tuple-element.30.refs_0_), channel_id=1, source_target_pairs={{0,14},{2,0},{4,2},{6,4},{8,6},{10,8},{12,10},{14,12},{16,18},{18,... | collective-permute-start | bytes 786440 | tf_op jit(solution)/shard_map/ppermute | solution.py:340
  21.5 0.0 copy-start.13
  21.5 0.9 copy-done.13
  22.4 0.8 copy-done.15
  23.2 1.2 terms.1
  24.4 0.0 collective-permute-done.1.refs_2_
  24.4 3.6 %collective-permute-done.2.refs_1_ = bf16[256,512]{1,0:T(8,128)(2,1)} collective-permute-done((bf16[256,512]{1,0:T(8,128)(2,1)S(1)}, bf16[256,512]{1,0:T(8,128)(2,1)}, u32[]{:S(2)}, u32[]{:S(2)}) %collective-permute-start.2) | collective-permute-done | bytes 262176 | tf_op jit(solution)/shard_map/ppermute | solution.py:340
  28.0 1.9 %collective-permute-start.5 = (bf16[16,2,16,512]{3,2,1,0:T(8,128)(2,1)S(1)}, bf16[16,2,16,512]{3,2,1,0:T(8,128)(2,1)S(1)}, u32[]{:S(2)}, u32[]{:S(2)}) collective-permute-start(bf16[16,2,16,512]{3,2,1,0:T(8,128)(2,1)S(1)} %get-tuple-element.37), channel_id=1, source_target_pairs={{0,16},{16,0},{1,17},{17,1},{2,18},{18,2},{3,19},{19,3},{4,20},{20... | collective-permute-start | bytes 1572872 | tf_op jit(solution)/shard_map/ppermute | solution.py:344
  29.9 4.6 %collective-permute-start = (bf16[8,256,256]{2,1,0:T(8,128)(2,1)}, bf16[8,256,256]{2,1,0:T(8,128)(2,1)S(1)}, u32[]{:S(2)}, u32[]{:S(2)}) collective-permute-start(bf16[8,256,256]{2,1,0:T(8,128)(2,1)} %dynamic-slice_bitcast_fusion), channel_id=1, source_target_pairs={{0,1},{1,0},{2,3},{3,2},{4,5},{5,4},{6,7},{7,6},{8,9},{9,8},{10,11... | collective-permute-start | bytes 3145736 | tf_op jit(solution)/shard_map/ppermute | solution.py:344
  34.5 3.7 %collective-permute-start.3 = (bf16[256,512]{1,0:T(8,128)(2,1)}, bf16[256,512]{1,0:T(8,128)(2,1)}, u32[]{:S(2)}, u32[]{:S(2)}) collective-permute-start(bf16[256,512]{1,0:T(8,128)(2,1)} %collective-permute-done.1.refs_2_), channel_id=1, source_target_pairs={{0,2},{2,4},{4,6},{6,8},{8,10},{10,12},{12,14},{14,0},{16,30},{18,... | collective-permute-start | bytes 786440 | tf_op jit(solution)/shard_map/ppermute | solution.py:340
  38.3 1.9 %collective-permute-start.4 = (bf16[256,512]{1,0:T(8,128)(2,1)}, bf16[256,512]{1,0:T(8,128)(2,1)}, u32[]{:S(2)}, u32[]{:S(2)}) collective-permute-start(bf16[256,512]{1,0:T(8,128)(2,1)} %collective-permute-done.2.refs_1_), channel_id=1, source_target_pairs={{0,14},{2,0},{4,2},{6,4},{8,6},{10,8},{12,10},{14,12},{16,18},{18,... | collective-permute-start | bytes 786440 | tf_op jit(solution)/shard_map/ppermute | solution.py:340
  40.2 2.1 %collective-permute-done.3.refs_4_ = bf16[256,512]{1,0:T(8,128)(2,1)} collective-permute-done((bf16[256,512]{1,0:T(8,128)(2,1)}, bf16[256,512]{1,0:T(8,128)(2,1)}, u32[]{:S(2)}, u32[]{:S(2)}) %collective-permute-start.3) | collective-permute-done | bytes 262176 | tf_op jit(solution)/shard_map/ppermute | solution.py:340
  42.3 5.2 %collective-permute-done.4.refs_3_ = bf16[256,512]{1,0:T(8,128)(2,1)} collective-permute-done((bf16[256,512]{1,0:T(8,128)(2,1)}, bf16[256,512]{1,0:T(8,128)(2,1)}, u32[]{:S(2)}, u32[]{:S(2)}) %collective-permute-start.4) | collective-permute-done | bytes 262176 | tf_op jit(solution)/shard_map/ppermute | solution.py:340
  47.4 0.0 collective-permute-done.5
  47.4 2.1 %collective-permute-start.6 = (bf16[256,512]{1,0:T(8,128)(2,1)}, bf16[256,512]{1,0:T(8,128)(2,1)}, u32[]{:S(2)}, u32[]{:S(2)}) collective-permute-start(bf16[256,512]{1,0:T(8,128)(2,1)} %collective-permute-done.3.refs_4_), channel_id=1, source_target_pairs={{0,2},{2,4},{4,6},{6,8},{8,10},{10,12},{12,14},{14,0},{16,30},{18,... | collective-permute-start | bytes 786440 | tf_op jit(solution)/shard_map/ppermute | solution.py:340
  49.6 3.1 %collective-permute-start.7 = (bf16[256,512]{1,0:T(8,128)(2,1)}, bf16[256,512]{1,0:T(8,128)(2,1)}, u32[]{:S(2)}, u32[]{:S(2)}) collective-permute-start(bf16[256,512]{1,0:T(8,128)(2,1)} %collective-permute-done.4.refs_3_), channel_id=1, source_target_pairs={{0,14},{2,0},{4,2},{6,4},{8,6},{10,8},{12,10},{14,12},{16,18},{18,... | collective-permute-start | bytes 786440 | tf_op jit(solution)/shard_map/ppermute | solution.py:340
  52.7 1.0 add_convert_fusion
  53.7 7.9 %all-to-all-start.1 = ((bf16[32,16,512]{2,1,0:T(8,128)(2,1)}), bf16[32,16,512]{2,1,0:T(8,128)(2,1)}, u32[]{:S(2)}, u32[]{:S(2)}) async-start(bf16[32,16,512]{2,1,0:T(8,128)(2,1)} %bitcast.43), calls=%async_computation.1 | async-start | bytes 1048576 | tf_op jit(solution)/shard_map/all_to_all | solution.py:407
  61.6 0.0 collective-permute-done.6.refs_1_
  61.6 0.0 collective-permute-done.7.refs_0_
  61.6 3.4 %collective-permute-start.8 = (bf16[256,512]{1,0:T(8,128)(2,1)}, bf16[256,512]{1,0:T(8,128)(2,1)}, u32[]{:S(2)}, u32[]{:S(2)}) collective-permute-start(bf16[256,512]{1,0:T(8,128)(2,1)} %collective-permute-done.6.refs_1_), channel_id=1, source_target_pairs={{0,2},{2,4},{4,6},{6,8},{8,10},{10,12},{12,14},{14,0},{16,30},{18,... | collective-permute-start | bytes 786440 | tf_op jit(solution)/shard_map/ppermute | solution.py:340
  65.0 0.1 stack.72.where
  65.1 0.1 stack.83.where
  65.2 0.1 pad_add_fusion.where
  65.3 0.0 collective-permute-done
  65.3 4.2 %fold.2.refs_2_ = f32[2,256,512]{2,1,0:T(8,128)S(1)} custom-call(s32[10]{0:T(128)S(1)} %stack.83.where, bf16[4096,256]{1,0:T(8,128)(2,1)S(1)} %copy-done, bf16[2048,256]{1,0:T(8,128)(2,1)S(1)} %bitcast.33, bf16[256,512]{1,0:T(8,128)(2,1)S(1)} %get-tuple-element.30.refs_0_, bf16[256,512]{1,0:T(8,128)(2,1)} %collective-permute-done.2.refs_1_, ...), custom_call_target="tpu_custom_call" | custom-call | flops 670000000 | bytes 3000000 | tf_op jit(solution)/shard_map/fold/pallas_call | solution.py:58
  69.5 3.0 %fold.3 = (f32[2,256,512]{2,1,0:T(8,128)S(1)}, bf16[2,256,256]{2,1,0:T(8,128)(2,1)S(1)}) custom-call(s32[6]{0:T(128)S(1)} %stack.72.where, bf16[4096,256]{1,0:T(8,128)(2,1)S(1)} %copy-done, bf16[2048,256]{1,0:T(8,128)(2,1)S(1)} %bitcast.34, bf16[256,512]{1,0:T(8,128)(2,1)} %collective-permute-done.7.refs_0_, ...), custom_call_target="tpu_custom_call" | custom-call | flops 268000000 | bytes 3000000 | tf_op jit(solution)/shard_map/fold/pallas_call | solution.py:58
  72.5 0.0 collective-permute-done.8.block
  72.5 1.3 last.1
  73.8 2.5 %collective-permute-start.9 = (bf16[2,128,512]{2,1,0:T(8,128)(2,1)S(1)}, bf16[2,128,512]{2,1,0:T(8,128)(2,1)S(1)}, u32[]{:S(2)}, u32[]{:S(2)}) collective-permute-start(bf16[2,128,512]{2,1,0:T(8,128)(2,1)S(1)} %get-tuple-element.45), channel_id=1, source_target_pairs={{0,16},{16,0},{1,17},{17,1},{2,18},{18,2},{3,19},{19,3},{4,20},{20... | collective-permute-start | bytes 786440 | tf_op jit(solution)/shard_map/ppermute | solution.py:344
  76.3 1.1 collective-permute-done.9
  77.4 0.8 add_convert_fusion.1
  78.2 0.0 all-to-all-done.1
  78.2 9.4 %all-to-all-start = ((bf16[32,8,512]{2,1,0:T(8,128)(2,1)}), bf16[32,8,512]{2,1,0:T(8,128)(2,1)S(1)}, u32[]{:S(2)}, u32[]{:S(2)}) async-start(bf16[32,8,512]{2,1,0:T(8,128)(2,1)} %bitcast.28), calls=%async_computation | async-start | bytes 524288 | tf_op jit(solution)/shard_map/all_to_all | solution.py:426
  87.6 1.1 convert_reduce_fusion
  88.8 2.1 %collective-permute-start.10 = (f32[16,512]{1,0:T(8,128)S(1)}, f32[16,512]{1,0:T(8,128)S(1)}, u32[]{:S(2)}, u32[]{:S(2)}) collective-permute-start(f32[16,512]{1,0:T(8,128)S(1)} %convert_reduce_fusion), channel_id=1, source_target_pairs={{0,2},{2,0},{4,6},{6,4},{8,10},{10,8},{12,14},{14,12},{1,3},{3,1},... | collective-permute-start | bytes 98312 | tf_op jit(solution)/shard_map/ppermute | solution.py:429
  90.9 2.8 %collective-permute-done.10 = f32[16,512]{1,0:T(8,128)S(1)} collective-permute-done((f32[16,512]{1,0:T(8,128)S(1)}, f32[16,512]{1,0:T(8,128)S(1)}, u32[]{:S(2)}, u32[]{:S(2)}) %collective-permute-start.10) | collective-permute-done | bytes 32800 | tf_op jit(solution)/shard_map/ppermute | solution.py:429
  93.7 3.4 %collective-permute-start.11 = (f32[16,512]{1,0:T(8,128)S(1)}, f32[16,512]{1,0:T(8,128)S(1)}, u32[]{:S(2)}, u32[]{:S(2)}) collective-permute-start(f32[16,512]{1,0:T(8,128)S(1)} %add.119), channel_id=1, source_target_pairs={{0,4},{2,6},{4,0},{6,2},{8,12},{10,14},{12,8},{14,10},{1,5},{3,7},... | collective-permute-start | bytes 98312 | tf_op jit(solution)/shard_map/ppermute | solution.py:429
  97.2 2.7 %collective-permute-done.11 = f32[16,512]{1,0:T(8,128)S(1)} collective-permute-done((f32[16,512]{1,0:T(8,128)S(1)}, f32[16,512]{1,0:T(8,128)S(1)}, u32[]{:S(2)}, u32[]{:S(2)}) %collective-permute-start.11) | collective-permute-done | bytes 32800 | tf_op jit(solution)/shard_map/ppermute | solution.py:429
  99.8 0.0 all-to-all-done
  99.8 0.1 reduce_sum.22
  99.9 0.7 broadcast_in_dim.18
  100.6 7.1 %all-to-all-start.2 = ((bf16[16,8,512]{2,1,0:T(8,128)(2,1)}), bf16[16,8,512]{2,1,0:T(8,128)(2,1)S(1)}, u32[]{:S(2)}, u32[]{:S(2)}) async-start(bf16[16,8,512]{2,1,0:T(8,128)(2,1)} %broadcast_in_dim.18), calls=%async_computation.2 | async-start | bytes 262144 | tf_op jit(solution)/shard_map/all_to_all | solution.py:352
  107.7 4.2 %collective-permute-start.12 = (f32[16,512]{1,0:T(8,128)S(1)}, f32[16,512]{1,0:T(8,128)S(1)}, u32[]{:S(2)}, u32[]{:S(2)}) collective-permute-start(f32[16,512]{1,0:T(8,128)S(1)} %add.120), channel_id=1, source_target_pairs={{0,8},{2,10},{4,12},{6,14},{8,0},{10,2},{12,4},{14,6},{1,9},{3,11}... | collective-permute-start | bytes 98312 | tf_op jit(solution)/shard_map/ppermute | solution.py:429
  111.9 4.3 %collective-permute-done.12 = f32[16,512]{1,0:T(8,128)S(1)} collective-permute-done((f32[16,512]{1,0:T(8,128)S(1)}, f32[16,512]{1,0:T(8,128)S(1)}, u32[]{:S(2)}, u32[]{:S(2)}) %collective-permute-start.12) | collective-permute-done | bytes 32800 | tf_op jit(solution)/shard_map/ppermute | solution.py:429
  116.3 4.4 %collective-permute-start.13 = (f32[16,512]{1,0:T(8,128)S(1)}, f32[16,512]{1,0:T(8,128)S(1)}, u32[]{:S(2)}, u32[]{:S(2)}) collective-permute-start(f32[16,512]{1,0:T(8,128)S(1)} %add.121), channel_id=1, source_target_pairs={{0,1},{1,0},{2,3},{3,2},{4,5},{5,4},{6,7},{7,6},{8,9},{9,8},{10,11... | collective-permute-start | bytes 98312 | tf_op jit(solution)/shard_map/ppermute | solution.py:344
  120.6 1.8 %collective-permute-done.13 = f32[16,512]{1,0:T(8,128)S(1)} collective-permute-done((f32[16,512]{1,0:T(8,128)S(1)}, f32[16,512]{1,0:T(8,128)S(1)}, u32[]{:S(2)}, u32[]{:S(2)}) %collective-permute-start.13) | collective-permute-done | bytes 32800 | tf_op jit(solution)/shard_map/ppermute | solution.py:344
  122.4 0.0 all-to-all-done.2
  122.4 7.1 %all_gather.3 = bf16[256,512]{1,0:T(8,128)(2,1)S(1)} all-gather(bf16[128,512]{1,0:T(8,128)(2,1)S(1)} %bitcast.44), channel_id=1, replica_groups=mesh['xl'=2,'y'=8,'c'=2,'z'=8,'xh'=2] {'c'}, dimensions={0}, use_global_device_ids=true | all-gather | bytes 393216 | tf_op jit(solution)/shard_map/all_gather | solution.py:439
  129.6 0.9 convert_element_type.25
  130.4 0.6 broadcast_select_fusion
  (22 shorter events, 0.1 us)
Async XLA Ops:
  0.6 2.5 %copy-start.11 = (s32[128]{0:T(128)S(1)}, s32[128]{0:T(128)}, u32[]{:S(2)}) copy-start(s32[128]{0:T(128)} %param.23) | copy-start | bytes 1540
  0.6 2.5 %copy-start.10 = (s32[256]{0:T(256)S(1)}, s32[256]{0:T(256)}, u32[]{:S(2)}) copy-start(s32[256]{0:T(256)} %param.21) | copy-start | bytes 3076
  0.7 2.5 %copy-start.9 = (s32[128,5]{0,1:T(8,128)S(1)}, s32[128,5]{0,1:T(8,128)}, u32[]{:S(2)}) copy-start(s32[128,5]{0,1:T(8,128)} %param.22) | copy-start | bytes 7684
  0.7 2.5 %copy-start.7 = (s32[256,10]{0,1:T(8,128)S(1)}, s32[256,10]{0,1:T(8,128)}, u32[]{:S(2)}) copy-start(s32[256,10]{0,1:T(8,128)} %param.20) | copy-start | bytes 30724
  0.7 2.5 %copy-start.3 = (s32[4096,15]{0,1:T(8,128)S(1)}, s32[4096,15]{0,1:T(8,128)}, u32[]{:S(2)}) copy-start(s32[4096,15]{0,1:T(8,128)} %param.18) | copy-start | bytes 737284
  0.7 2.5 %copy-start.8 = (s32[4096]{0:T(1024)S(1)}, s32[4096]{0:T(1024)}, u32[]{:S(2)}) copy-start(s32[4096]{0:T(1024)} %param.19) | copy-start | bytes 49156
  0.7 2.5 %copy-start.5 = (bf16[256,512]{1,0:T(8,128)(2,1)S(1)}, bf16[256,512]{1,0:T(8,128)(2,1)}, u32[]{:S(2)}) copy-start(bf16[256,512]{1,0:T(8,128)(2,1)} %pre_one_hbm.3) | copy-start | bytes 786436
  0.7 2.5 %copy-start.4 = (bf16[256,512]{1,0:T(8,128)(2,1)S(1)}, bf16[256,512]{1,0:T(8,128)(2,1)}, u32[]{:S(2)}) copy-start(bf16[256,512]{1,0:T(8,128)(2,1)} %pre_two_hbm.3) | copy-start | bytes 786436
  0.7 2.5 %copy-start.6 = (bf16[128,512]{1,0:T(8,128)(2,1)S(1)}, bf16[128,512]{1,0:T(8,128)(2,1)}, u32[]{:S(2)}) copy-start(bf16[128,512]{1,0:T(8,128)(2,1)} %cotangent_hbm.3) | copy-start | bytes 393220
  0.7 2.5 %copy-start.2 = (bf16[512,512]{1,0:T(8,128)(2,1)S(1)}, bf16[512,512]{1,0:T(8,128)(2,1)}, u32[]{:S(2)}) copy-start(bf16[512,512]{1,0:T(8,128)(2,1)} %weight_two_hbm.1) | copy-start | bytes 1572868
  0.7 2.5 %copy-start.1 = (bf16[512,512]{1,0:T(8,128)(2,1)S(1)}, bf16[512,512]{1,0:T(8,128)(2,1)}, u32[]{:S(2)}) copy-start(bf16[512,512]{1,0:T(8,128)(2,1)} %weight_three_hbm.1) | copy-start | bytes 1572868
  6.7 0.7 copy-start.12
  7.4 0.6 copy-start.14
  8.0 16.3 %collective-permute-start.1 = (bf16[256,512]{1,0:T(8,128)(2,1)S(1)}, bf16[256,512]{1,0:T(8,128)(2,1)}, u32[]{:S(2)}, u32[]{:S(2)}) collective-permute-start(bf16[256,512]{1,0:T(8,128)(2,1)S(1)} %get-tuple-element.30.refs_0_), channel_id=1, source_target_pairs={{0,2},{2,4},{4,6},{6,8},{8,10},{10,12},{12,14},{14,0},{16,30},{18,... | collective-permute-start | bytes 786440 | tf_op jit(solution)/shard_map/ppermute | solution.py:340
  19.5 8.4 %collective-permute-start.2 = (bf16[256,512]{1,0:T(8,128)(2,1)S(1)}, bf16[256,512]{1,0:T(8,128)(2,1)}, u32[]{:S(2)}, u32[]{:S(2)}) collective-permute-start(bf16[256,512]{1,0:T(8,128)(2,1)S(1)} %get-tuple-element.30.refs_0_), channel_id=1, source_target_pairs={{0,14},{2,0},{4,2},{6,4},{8,6},{10,8},{12,10},{14,12},{16,18},{18,... | collective-permute-start | bytes 786440 | tf_op jit(solution)/shard_map/ppermute | solution.py:340
  21.5 0.9 copy-start.13
  22.4 0.8 copy-start.15
  23.2 42.1 %copy-start = (bf16[4096,256]{1,0:T(8,128)(2,1)S(1)}, bf16[4096,256]{1,0:T(8,128)(2,1)}, u32[]{:S(2)}) copy-start(bf16[4096,256]{1,0:T(8,128)(2,1)} %features_hbm.3) | copy-start | bytes 6291460
  28.0 19.5 %collective-permute-start.5 = (bf16[16,2,16,512]{3,2,1,0:T(8,128)(2,1)S(1)}, bf16[16,2,16,512]{3,2,1,0:T(8,128)(2,1)S(1)}, u32[]{:S(2)}, u32[]{:S(2)}) collective-permute-start(bf16[16,2,16,512]{3,2,1,0:T(8,128)(2,1)S(1)} %get-tuple-element.37), channel_id=1, source_target_pairs={{0,16},{16,0},{1,17},{17,1},{2,18},{18,2},{3,19},{19,3},{4,20},{20... | collective-permute-start | bytes 1572872 | tf_op jit(solution)/shard_map/ppermute | solution.py:344
  29.9 35.4 %collective-permute-start = (bf16[8,256,256]{2,1,0:T(8,128)(2,1)}, bf16[8,256,256]{2,1,0:T(8,128)(2,1)S(1)}, u32[]{:S(2)}, u32[]{:S(2)}) collective-permute-start(bf16[8,256,256]{2,1,0:T(8,128)(2,1)} %dynamic-slice_bitcast_fusion), channel_id=1, source_target_pairs={{0,1},{1,0},{2,3},{3,2},{4,5},{5,4},{6,7},{7,6},{8,9},{9,8},{10,11... | collective-permute-start | bytes 3145736 | tf_op jit(solution)/shard_map/ppermute | solution.py:344
  34.5 7.7 %collective-permute-start.3 = (bf16[256,512]{1,0:T(8,128)(2,1)}, bf16[256,512]{1,0:T(8,128)(2,1)}, u32[]{:S(2)}, u32[]{:S(2)}) collective-permute-start(bf16[256,512]{1,0:T(8,128)(2,1)} %collective-permute-done.1.refs_2_), channel_id=1, source_target_pairs={{0,2},{2,4},{4,6},{6,8},{8,10},{10,12},{12,14},{14,0},{16,30},{18,... | collective-permute-start | bytes 786440 | tf_op jit(solution)/shard_map/ppermute | solution.py:340
  38.3 9.1 %collective-permute-start.4 = (bf16[256,512]{1,0:T(8,128)(2,1)}, bf16[256,512]{1,0:T(8,128)(2,1)}, u32[]{:S(2)}, u32[]{:S(2)}) collective-permute-start(bf16[256,512]{1,0:T(8,128)(2,1)} %collective-permute-done.2.refs_1_), channel_id=1, source_target_pairs={{0,14},{2,0},{4,2},{6,4},{8,6},{10,8},{12,10},{14,12},{16,18},{18,... | collective-permute-start | bytes 786440 | tf_op jit(solution)/shard_map/ppermute | solution.py:340
  47.4 14.2 %collective-permute-start.6 = (bf16[256,512]{1,0:T(8,128)(2,1)}, bf16[256,512]{1,0:T(8,128)(2,1)}, u32[]{:S(2)}, u32[]{:S(2)}) collective-permute-start(bf16[256,512]{1,0:T(8,128)(2,1)} %collective-permute-done.3.refs_4_), channel_id=1, source_target_pairs={{0,2},{2,4},{4,6},{6,8},{8,10},{10,12},{12,14},{14,0},{16,30},{18,... | collective-permute-start | bytes 786440 | tf_op jit(solution)/shard_map/ppermute | solution.py:340
  49.6 12.1 %collective-permute-start.7 = (bf16[256,512]{1,0:T(8,128)(2,1)}, bf16[256,512]{1,0:T(8,128)(2,1)}, u32[]{:S(2)}, u32[]{:S(2)}) collective-permute-start(bf16[256,512]{1,0:T(8,128)(2,1)} %collective-permute-done.4.refs_3_), channel_id=1, source_target_pairs={{0,14},{2,0},{4,2},{6,4},{8,6},{10,8},{12,10},{14,12},{16,18},{18,... | collective-permute-start | bytes 786440 | tf_op jit(solution)/shard_map/ppermute | solution.py:340
  53.7 24.5 %all-to-all-start.1 = ((bf16[32,16,512]{2,1,0:T(8,128)(2,1)}), bf16[32,16,512]{2,1,0:T(8,128)(2,1)}, u32[]{:S(2)}, u32[]{:S(2)}) async-start(bf16[32,16,512]{2,1,0:T(8,128)(2,1)} %bitcast.43), calls=%async_computation.1 | async-start | bytes 1048576 | tf_op jit(solution)/shard_map/all_to_all | solution.py:407
  61.6 10.9 %collective-permute-start.8 = (bf16[256,512]{1,0:T(8,128)(2,1)}, bf16[256,512]{1,0:T(8,128)(2,1)}, u32[]{:S(2)}, u32[]{:S(2)}) collective-permute-start(bf16[256,512]{1,0:T(8,128)(2,1)} %collective-permute-done.6.refs_1_), channel_id=1, source_target_pairs={{0,2},{2,4},{4,6},{6,8},{8,10},{10,12},{12,14},{14,0},{16,30},{18,... | collective-permute-start | bytes 786440 | tf_op jit(solution)/shard_map/ppermute | solution.py:340
  73.8 3.6 %collective-permute-start.9 = (bf16[2,128,512]{2,1,0:T(8,128)(2,1)S(1)}, bf16[2,128,512]{2,1,0:T(8,128)(2,1)S(1)}, u32[]{:S(2)}, u32[]{:S(2)}) collective-permute-start(bf16[2,128,512]{2,1,0:T(8,128)(2,1)S(1)} %get-tuple-element.45), channel_id=1, source_target_pairs={{0,16},{16,0},{1,17},{17,1},{2,18},{18,2},{3,19},{19,3},{4,20},{20... | collective-permute-start | bytes 786440 | tf_op jit(solution)/shard_map/ppermute | solution.py:344
  78.2 21.6 %all-to-all-start = ((bf16[32,8,512]{2,1,0:T(8,128)(2,1)}), bf16[32,8,512]{2,1,0:T(8,128)(2,1)S(1)}, u32[]{:S(2)}, u32[]{:S(2)}) async-start(bf16[32,8,512]{2,1,0:T(8,128)(2,1)} %bitcast.28), calls=%async_computation | async-start | bytes 524288 | tf_op jit(solution)/shard_map/all_to_all | solution.py:426
  88.8 5.0 %collective-permute-start.10 = (f32[16,512]{1,0:T(8,128)S(1)}, f32[16,512]{1,0:T(8,128)S(1)}, u32[]{:S(2)}, u32[]{:S(2)}) collective-permute-start(f32[16,512]{1,0:T(8,128)S(1)} %convert_reduce_fusion), channel_id=1, source_target_pairs={{0,2},{2,0},{4,6},{6,4},{8,10},{10,8},{12,14},{14,12},{1,3},{3,1},... | collective-permute-start | bytes 98312 | tf_op jit(solution)/shard_map/ppermute | solution.py:429
  93.7 6.1 %collective-permute-start.11 = (f32[16,512]{1,0:T(8,128)S(1)}, f32[16,512]{1,0:T(8,128)S(1)}, u32[]{:S(2)}, u32[]{:S(2)}) collective-permute-start(f32[16,512]{1,0:T(8,128)S(1)} %add.119), channel_id=1, source_target_pairs={{0,4},{2,6},{4,0},{6,2},{8,12},{10,14},{12,8},{14,10},{1,5},{3,7},... | collective-permute-start | bytes 98312 | tf_op jit(solution)/shard_map/ppermute | solution.py:429
  100.6 21.9 %all-to-all-start.2 = ((bf16[16,8,512]{2,1,0:T(8,128)(2,1)}), bf16[16,8,512]{2,1,0:T(8,128)(2,1)S(1)}, u32[]{:S(2)}, u32[]{:S(2)}) async-start(bf16[16,8,512]{2,1,0:T(8,128)(2,1)} %broadcast_in_dim.18), calls=%async_computation.2 | async-start | bytes 262144 | tf_op jit(solution)/shard_map/all_to_all | solution.py:352
  107.7 8.6 %collective-permute-start.12 = (f32[16,512]{1,0:T(8,128)S(1)}, f32[16,512]{1,0:T(8,128)S(1)}, u32[]{:S(2)}, u32[]{:S(2)}) collective-permute-start(f32[16,512]{1,0:T(8,128)S(1)} %add.120), channel_id=1, source_target_pairs={{0,8},{2,10},{4,12},{6,14},{8,0},{10,2},{12,4},{14,6},{1,9},{3,11}... | collective-permute-start | bytes 98312 | tf_op jit(solution)/shard_map/ppermute | solution.py:429
  116.3 6.2 %collective-permute-start.13 = (f32[16,512]{1,0:T(8,128)S(1)}, f32[16,512]{1,0:T(8,128)S(1)}, u32[]{:S(2)}, u32[]{:S(2)}) collective-permute-start(f32[16,512]{1,0:T(8,128)S(1)} %add.121), channel_id=1, source_target_pairs={{0,1},{1,0},{2,3},{3,2},{4,5},{5,4},{6,7},{7,6},{8,9},{9,8},{10,11... | collective-permute-start | bytes 98312 | tf_op jit(solution)/shard_map/ppermute | solution.py:344

commit v3 on v2

--- a/solution.py
+++ b/solution.py
@@ -301,34 +301,24 @@
     )
 
 
-def run_last(total, last, block, core, half):
-    width = total.shape[1]
-    rows = width // 2
-    where = jnp.stack([core, half]).astype(jnp.int32)
-
-    def kernel(where, total, last, block, sent, kept, scratch):
-        core, half = where[0], where[1]
-        keep = pl.multiple_of(core * rows, rows)
-        send = pl.multiple_of((1 - core) * rows, rows)
+def run_last(total, last, block, half):
+    where = jnp.reshape(half, (1,)).astype(jnp.int32)
+
+    def kernel(where, total, last, block, sent):
         for side in range(2):
-            scratch[...] = total[side] + mul(last[side], block[...], 1, 0)
-            place = half if side == 0 else 1 - half
-            kept[place] = scratch[pl.ds(keep, rows), :]
-            sent[place] = scratch[pl.ds(send, rows), :].astype(BF)
+            place = where[0] if side == 0 else 1 - where[0]
+            sent[place] = (total[side] + mul(last[side], block[...], 1, 0)).astype(BF)
 
     return call(
         kernel,
         "last",
-        (
-            jax.ShapeDtypeStruct((2, rows, HIDDEN), BF),
-            jax.ShapeDtypeStruct((2, rows, HIDDEN), F32),
-        ),
+        (jax.ShapeDtypeStruct(total.shape, BF),),
         [IN_SMEM] + [IN_VMEM] * 3,
-        [pltpu.VMEM((width, HIDDEN), F32)],
+        [],
         2 * 70_000_000,
         16,
         [where, total, last, block],
-    )
+    )[0]
 
 
 def turn(block, sign):
@@ -421,9 +411,8 @@
     total, last = run_fold(
         features, theirs, [behind[3], ahead[3]], *places([3, -3, -4]), total
     )
-    sent, kept = run_last(total, last, ahead[4], c, xh)
-    total = (kept + swap(sent, "c").astype(F32)).astype(BF).reshape(32, 8, HIDDEN)
-    total = lax.all_to_all(total, ("xh", "xl", "y"), 0, 0)
+    total = run_last(total, last, ahead[4], xh).reshape(64, 8, HIDDEN)
+    total = lax.all_to_all(total, ("xh", "c", "xl", "y"), 0, 0)
 
     def double(terms, step):
         return terms + lax.ppermute(terms, "z", [(k, k ^ step) for k in range(Z)])
@@ -432,11 +421,10 @@
     terms = double(double(terms, 1), 2)
     total, terms = after(total, terms)
     total = jnp.sum(total.astype(F32), axis=0).astype(BF)
-    total = spread_out(total, ("xl", "y"), 16).reshape(width // 2, HIDDEN)
+    total = spread_out(total, ("c", "xl", "y"), 32).reshape(width, HIDDEN)
     terms = double(terms, 4)
     other = swap(terms, "xh")
-    total, terms, other = after(total, terms, other)
-    grad_one = lax.all_gather(total, "c", axis=0, tiled=True).astype(F32)
+    grad_one = total.astype(F32)
     grad_two = jnp.where(xh == 0, terms, other)
     grad_three = jnp.where(xh == 0, other, terms)
     return (grad_one, grad_two, grad_three)

time: 132 us -> 131 us (level)
  waiting for transfers between devices: 23.6 us -> 35.4 us
  blocking collectives: 7.14 us -> 0 us
  starting transfers between devices: 75.3 us -> 71.6 us
  local copies, waits for them, and re-layouts: 6.31 us -> 4.07 us
    all_to_all x1, waiting for transfers between devices: 0.01 us -> 7.3 us  [body(): total = lax.all_to_all(total, ('xh', 'c', 'xl', 'y'), 0, 0)]
    all_gather x1 -> x0, blocking collectives: 7.14 us -> none  [body(): grad_one = lax.all_gather(total, 'c', axis=0, tiled=True).astype(F32)]
    ppermute x4 -> x3, starting transfers between devices: 13.4 us -> 9.54 us  [swap(): return lax.ppermute(block, axis, [(0, 1), (1, 0)])]
    ppermute x7, waiting for transfers between devices: 10.8 us -> 14.4 us  [turn(): return lax.ppermute(block, ('c', 'z'), pairs)]
    all_to_all x1, starting transfers between devices: 7.13 us -> 3.66 us  [spread_out(): lax.all_to_all(jnp.broadcast_to(piece[None], (count,) + piece.shape), axe...]
    all_to_all x1, starting transfers between devices: 9.42 us -> 12.3 us  [body(): total = lax.all_to_all(total, ('xh', 'c', 'xl', 'y'), 0, 0)]
    unnamed x32 -> x28, local copies, waits for them, and re-layouts: 3.06 us -> 0.76 us
    all_to_all x1, starting transfers between devices: 7.92 us -> 9.81 us  [body(): terms = lax.all_to_all(terms, ('xl', 'y', 'xh'), 0, 0)]
  transfers between devices with their start and end apart: 17 -> 16, of which waited for: 8 -> 10; matrix products, arithmetic and copies ran while one was open for 2% -> 2% of each run, Pallas kernels for 7% -> 8%
where the time goes in v3:
time: 131 us; the launch traced here: 130 us
  starting transfers between devices  71.6 us (55%)
  waiting for transfers between devices  35.4 us (27%)
  Pallas kernels  13.8 us (11%)
  local copies, waits for them, and re-layouts  4.07 us (3%)
  other arithmetic  3.74 us (3%)
    ppermute x7, starting transfers between devices, turn(): return lax.ppermute(block, ('c', 'z'), pairs)  26.8 us
    ppermute x7, waiting for transfers between devices, turn(): return lax.ppermute(block, ('c', 'z'), pairs)  14.4 us
    pallas_call x5, Pallas kernels, call(): pl.pallas_call(kernel, out_shape=out_shape, in_specs=in_specs, out_specs=...  13.8 us
    all_to_all x1, starting transfers between devices, body(): total = lax.all_to_all(total, ('xh', 'c', 'xl', 'y'), 0, 0)  12.3 us
    ppermute x3, waiting for transfers between devices, double(): return terms + lax.ppermute(terms, 'z', [(k, k ^ step) for k in range(Z)])  10.6 us
    all_to_all x1, starting transfers between devices, body(): terms = lax.all_to_all(terms, ('xl', 'y', 'xh'), 0, 0)  9.81 us
    ppermute x3, starting transfers between devices, swap(): return lax.ppermute(block, axis, [(0, 1), (1, 0)])  9.54 us
    ppermute x3, starting transfers between devices, double(): return terms + lax.ppermute(terms, 'z', [(k, k ^ step) for k in range(Z)])  9.5 us
  transfers between devices with their start and end apart: 16, of which 10 were waited for; matrix products, arithmetic and copies ran while one was open for 2% of the time, Pallas kernels for 8%

profile of v3, /device:TPU:1, one launch (start us, length us, event | category | flops | bytes accessed | tf_op | source)
XLA Modules:
  0.0 129.7 jit_solution(17817911497650690540)
XLA Ops:
  0.6 0.0 copy-start.13
  0.6 0.0 copy-start.12
  0.7 0.0 copy-start.11
  0.7 0.0 copy-start.9
  0.7 0.0 copy-start.3
  0.7 0.0 copy-start.10
  0.7 0.0 copy-start.5
  0.7 0.0 copy-start.4
  0.7 0.0 copy-start.8
  0.7 0.0 copy-start.2
  0.7 0.0 copy-start.1
  0.8 2.4 %dynamic-slice_bitcast_fusion = bf16[8,256,256]{2,1,0:T(8,128)(2,1)} fusion(bf16[8,2,256,256]{3,2,1,0:T(8,128)(2,1)} %bitcast.34, s32[]{:T(128)S(6)} %select_n.16), kind=kLoop, calls=%fused_computation.2 | loop fusion | bytes 2097156 | tf_op jit(solution)/shard_map/jit(dynamic_index_in_dim)/squeeze | solution.py:366
  3.2 0.0 copy-done.13
  3.2 0.0 copy-done.12
  3.2 0.0 copy-done.11
  3.3 3.5 %chain.1 = (bf16[256,512]{1,0:T(8,128)(2,1)S(1)}, bf16[256,512]{1,0:T(8,128)(2,1)S(1)}, bf16[256,256]{1,0:T(8,128)(2,1)S(1)}, bf16[256,128]{1,0:T(8,128)(2,1)S(1)}) custom-call(s32[1]{0:T(128)} %bitcast.7.own, bf16[512,512]{1,0:T(8,128)(2,1)S(1)} %copy-done.1, bf16[128,512]{1,0:T(8,128)(2,1)S(1)} %copy-done.8, s32[5,128]{1,0:T(8,128)S(1)} %bitcast.40, ...), custom_call_target="tpu_custom_call" | custom-call | flops 436000000 | bytes 3000000 | tf_op jit(solution)/shard_map/chain/pallas_call | solution.py:58
  6.7 11.5 %collective-permute-start.1 = (bf16[256,512]{1,0:T(8,128)(2,1)S(1)}, bf16[256,512]{1,0:T(8,128)(2,1)}, u32[]{:S(2)}, u32[]{:S(2)}) collective-permute-start(bf16[256,512]{1,0:T(8,128)(2,1)S(1)} %get-tuple-element.25.refs_0_), channel_id=1, source_target_pairs={{0,2},{2,4},{4,6},{6,8},{8,10},{10,12},{12,14},{14,0},{16,30},{18,... | collective-permute-start | bytes 786440 | tf_op jit(solution)/shard_map/ppermute | solution.py:330
  18.3 1.9 %collective-permute-start.2 = (bf16[256,512]{1,0:T(8,128)(2,1)S(1)}, bf16[256,512]{1,0:T(8,128)(2,1)}, u32[]{:S(2)}, u32[]{:S(2)}) collective-permute-start(bf16[256,512]{1,0:T(8,128)(2,1)S(1)} %get-tuple-element.25.refs_0_), channel_id=1, source_target_pairs={{0,14},{2,0},{4,2},{6,4},{8,6},{10,8},{12,10},{14,12},{16,18},{18,... | collective-permute-start | bytes 786440 | tf_op jit(solution)/shard_map/ppermute | solution.py:330
  20.2 0.0 copy-start
  20.2 1.2 terms.1
  21.4 0.2 collective-permute-done.1.refs_2_
  21.6 5.1 %collective-permute-done.2.refs_1_ = bf16[256,512]{1,0:T(8,128)(2,1)} collective-permute-done((bf16[256,512]{1,0:T(8,128)(2,1)S(1)}, bf16[256,512]{1,0:T(8,128)(2,1)}, u32[]{:S(2)}, u32[]{:S(2)}) %collective-permute-start.2) | collective-permute-done | bytes 262176 | tf_op jit(solution)/shard_map/ppermute | solution.py:330
  26.7 1.9 %collective-permute-start.5 = (bf16[16,2,16,512]{3,2,1,0:T(8,128)(2,1)S(1)}, bf16[16,2,16,512]{3,2,1,0:T(8,128)(2,1)S(1)}, u32[]{:S(2)}, u32[]{:S(2)}) collective-permute-start(bf16[16,2,16,512]{3,2,1,0:T(8,128)(2,1)S(1)} %get-tuple-element.32), channel_id=1, source_target_pairs={{0,16},{16,0},{1,17},{17,1},{2,18},{18,2},{3,19},{19,3},{4,20},{20... | collective-permute-start | bytes 1572872 | tf_op jit(solution)/shard_map/ppermute | solution.py:334
  28.6 3.7 %collective-permute-start.3 = (bf16[256,512]{1,0:T(8,128)(2,1)}, bf16[256,512]{1,0:T(8,128)(2,1)}, u32[]{:S(2)}, u32[]{:S(2)}) collective-permute-start(bf16[256,512]{1,0:T(8,128)(2,1)} %collective-permute-done.1.refs_2_), channel_id=1, source_target_pairs={{0,2},{2,4},{4,6},{6,8},{8,10},{10,12},{12,14},{14,0},{16,30},{18,... | collective-permute-start | bytes 786440 | tf_op jit(solution)/shard_map/ppermute | solution.py:330
  32.3 1.9 %collective-permute-start.4 = (bf16[256,512]{1,0:T(8,128)(2,1)}, bf16[256,512]{1,0:T(8,128)(2,1)}, u32[]{:S(2)}, u32[]{:S(2)}) collective-permute-start(bf16[256,512]{1,0:T(8,128)(2,1)} %collective-permute-done.2.refs_1_), channel_id=1, source_target_pairs={{0,14},{2,0},{4,2},{6,4},{8,6},{10,8},{12,10},{14,12},{16,18},{18,... | collective-permute-start | bytes 786440 | tf_op jit(solution)/shard_map/ppermute | solution.py:330
  34.3 4.7 %collective-permute-start = (bf16[8,256,256]{2,1,0:T(8,128)(2,1)}, bf16[8,256,256]{2,1,0:T(8,128)(2,1)S(1)}, u32[]{:S(2)}, u32[]{:S(2)}) collective-permute-start(bf16[8,256,256]{2,1,0:T(8,128)(2,1)} %dynamic-slice_bitcast_fusion), channel_id=1, source_target_pairs={{0,1},{1,0},{2,3},{3,2},{4,5},{5,4},{6,7},{7,6},{8,9},{9,8},{10,11... | collective-permute-start | bytes 3145736 | tf_op jit(solution)/shard_map/ppermute | solution.py:334
  38.9 0.0 collective-permute-done.3.refs_4_
  39.0 2.1 %collective-permute-done.4.refs_3_ = bf16[256,512]{1,0:T(8,128)(2,1)} collective-permute-done((bf16[256,512]{1,0:T(8,128)(2,1)}, bf16[256,512]{1,0:T(8,128)(2,1)}, u32[]{:S(2)}, u32[]{:S(2)}) %collective-permute-start.4) | collective-permute-done | bytes 262176 | tf_op jit(solution)/shard_map/ppermute | solution.py:330
  41.0 0.0 collective-permute-done.5
  41.0 1.0 add_convert_fusion
  42.0 9.8 %all-to-all-start.1 = ((bf16[32,16,512]{2,1,0:T(8,128)(2,1)}), bf16[32,16,512]{2,1,0:T(8,128)(2,1)}, u32[]{:S(2)}, u32[]{:S(2)}) async-start(bf16[32,16,512]{2,1,0:T(8,128)(2,1)} %bitcast.45), calls=%async_computation.1 | async-start | bytes 1048576 | tf_op jit(solution)/shard_map/all_to_all | solution.py:397
  51.8 2.3 %collective-permute-start.6 = (bf16[256,512]{1,0:T(8,128)(2,1)}, bf16[256,512]{1,0:T(8,128)(2,1)}, u32[]{:S(2)}, u32[]{:S(2)}) collective-permute-start(bf16[256,512]{1,0:T(8,128)(2,1)} %collective-permute-done.3.refs_4_), channel_id=1, source_target_pairs={{0,2},{2,4},{4,6},{6,8},{8,10},{10,12},{12,14},{14,0},{16,30},{18,... | collective-permute-start | bytes 786440 | tf_op jit(solution)/shard_map/ppermute | solution.py:330
  54.2 3.0 %collective-permute-start.7 = (bf16[256,512]{1,0:T(8,128)(2,1)}, bf16[256,512]{1,0:T(8,128)(2,1)S(1)}, u32[]{:S(2)}, u32[]{:S(2)}) collective-permute-start(bf16[256,512]{1,0:T(8,128)(2,1)} %collective-permute-done.4.refs_3_), channel_id=1, source_target_pairs={{0,14},{2,0},{4,2},{6,4},{8,6},{10,8},{12,10},{14,12},{16,18},{18,... | collective-permute-start | bytes 786440 | tf_op jit(solution)/shard_map/ppermute | solution.py:330
  57.1 2.7 %collective-permute-done.6.refs_1_ = bf16[256,512]{1,0:T(8,128)(2,1)} collective-permute-done((bf16[256,512]{1,0:T(8,128)(2,1)}, bf16[256,512]{1,0:T(8,128)(2,1)}, u32[]{:S(2)}, u32[]{:S(2)}) %collective-permute-start.6) | collective-permute-done | bytes 262176 | tf_op jit(solution)/shard_map/ppermute | solution.py:330
  59.8 4.3 %collective-permute-done.7.refs_0_ = bf16[256,512]{1,0:T(8,128)(2,1)S(1)} collective-permute-done((bf16[256,512]{1,0:T(8,128)(2,1)}, bf16[256,512]{1,0:T(8,128)(2,1)S(1)}, u32[]{:S(2)}, u32[]{:S(2)}) %collective-permute-start.7) | collective-permute-done | bytes 262176 | tf_op jit(solution)/shard_map/ppermute | solution.py:330
  64.1 0.7 copy-done.6
  64.8 2.4 %collective-permute-start.8 = (bf16[256,512]{1,0:T(8,128)(2,1)}, bf16[256,512]{1,0:T(8,128)(2,1)}, u32[]{:S(2)}, u32[]{:S(2)}) collective-permute-start(bf16[256,512]{1,0:T(8,128)(2,1)} %collective-permute-done.6.refs_1_), channel_id=1, source_target_pairs={{0,2},{2,4},{4,6},{6,8},{8,10},{10,12},{12,14},{14,0},{16,30},{18,... | collective-permute-start | bytes 786440 | tf_op jit(solution)/shard_map/ppermute | solution.py:330
  67.3 0.1 stack.60.where
  67.4 0.1 stack.71.where
  67.5 0.0 collective-permute-done
  67.5 0.0 copy-done
  67.5 0.0 copy-start.7
  67.5 4.2 %fold.2.refs_2_ = f32[2,256,512]{2,1,0:T(8,128)S(1)} custom-call(s32[10]{0:T(128)S(1)} %stack.71.where, bf16[4096,256]{1,0:T(8,128)(2,1)S(1)} %copy-done, bf16[2048,256]{1,0:T(8,128)(2,1)S(1)} %bitcast.35, bf16[256,512]{1,0:T(8,128)(2,1)S(1)} %get-tuple-element.25.refs_0_, bf16[256,512]{1,0:T(8,128)(2,1)} %collective-permute-done.2.refs_1_, ...), custom_call_target="tpu_custom_call" | custom-call | flops 670000000 | bytes 3000000 | tf_op jit(solution)/shard_map/fold/pallas_call | solution.py:58
  71.7 2.9 %fold.3 = (f32[2,256,512]{2,1,0:T(8,128)S(1)}, bf16[2,256,256]{2,1,0:T(8,128)(2,1)S(1)}) custom-call(s32[6]{0:T(128)S(1)} %stack.60.where, bf16[4096,256]{1,0:T(8,128)(2,1)S(1)} %copy-done, bf16[2048,256]{1,0:T(8,128)(2,1)S(1)} %bitcast.36, bf16[256,512]{1,0:T(8,128)(2,1)S(1)} %copy-done.7, bf16[256,512]{1,0:T(8,128)(2,1)} %collective-permute-done.6.refs_1_, ...), custom_call_target="tpu_custom_call" | custom-call | flops 268000000 | bytes 3000000 | tf_op jit(solution)/shard_map/fold/pallas_call | solution.py:58
  74.7 0.0 collective-permute-done.8.block
  74.7 2.0 %last.1 = bf16[2,256,512]{2,1,0:T(8,128)(2,1)} custom-call(s32[1]{0:T(128)} %bitcast.where, f32[2,256,512]{2,1,0:T(8,128)S(1)} %get-tuple-element.37.total, bf16[2,256,256]{2,1,0:T(8,128)(2,1)S(1)} %get-tuple-element.38.last, bf16[256,512]{1,0:T(8,128)(2,1)} %collective-permute-done.8.block), custom_call_target="tpu_custom_call" | custom-call | flops 140000000 | bytes 3000000 | tf_op jit(solution)/shard_map/last/pallas_call | solution.py:58
  76.7 0.0 all-to-all-done.1
  76.7 12.3 %all-to-all-start = ((bf16[64,8,512]{2,1,0:T(8,128)(2,1)}), bf16[64,8,512]{2,1,0:T(8,128)(2,1)S(1)}, u32[]{:S(2)}, u32[]{:S(2)}) async-start(bf16[64,8,512]{2,1,0:T(8,128)(2,1)} %bitcast.28), calls=%async_computation | async-start | bytes 1048576 | tf_op jit(solution)/shard_map/all_to_all | solution.py:415
  89.0 1.1 convert_reduce_fusion
  90.2 1.9 %collective-permute-start.9 = (f32[16,512]{1,0:T(8,128)S(1)}, f32[16,512]{1,0:T(8,128)S(1)}, u32[]{:S(2)}, u32[]{:S(2)}) collective-permute-start(f32[16,512]{1,0:T(8,128)S(1)} %convert_reduce_fusion), channel_id=1, source_target_pairs={{0,2},{2,0},{4,6},{6,4},{8,10},{10,8},{12,14},{14,12},{1,3},{3,1},... | collective-permute-start | bytes 98312 | tf_op jit(solution)/shard_map/ppermute | solution.py:418
  92.1 3.0 %collective-permute-done.9 = f32[16,512]{1,0:T(8,128)S(1)} collective-permute-done((f32[16,512]{1,0:T(8,128)S(1)}, f32[16,512]{1,0:T(8,128)S(1)}, u32[]{:S(2)}, u32[]{:S(2)}) %collective-permute-start.9) | collective-permute-done | bytes 32800 | tf_op jit(solution)/shard_map/ppermute | solution.py:418
  95.1 2.9 %collective-permute-start.10 = (f32[16,512]{1,0:T(8,128)S(1)}, f32[16,512]{1,0:T(8,128)S(1)}, u32[]{:S(2)}, u32[]{:S(2)}) collective-permute-start(f32[16,512]{1,0:T(8,128)S(1)} %add.115), channel_id=1, source_target_pairs={{0,4},{2,6},{4,0},{6,2},{8,12},{10,14},{12,8},{14,10},{1,5},{3,7},... | collective-permute-start | bytes 98312 | tf_op jit(solution)/shard_map/ppermute | solution.py:418
  98.1 3.1 %collective-permute-done.10 = f32[16,512]{1,0:T(8,128)S(1)} collective-permute-done((f32[16,512]{1,0:T(8,128)S(1)}, f32[16,512]{1,0:T(8,128)S(1)}, u32[]{:S(2)}, u32[]{:S(2)}) %collective-permute-start.10) | collective-permute-done | bytes 32800 | tf_op jit(solution)/shard_map/ppermute | solution.py:418
  101.2 7.3 %all-to-all-done = bf16[64,8,512]{2,1,0:T(8,128)(2,1)S(1)} async-done(((bf16[64,8,512]{2,1,0:T(8,128)(2,1)}), bf16[64,8,512]{2,1,0:T(8,128)(2,1)S(1)}, u32[]{:S(2)}, u32[]{:S(2)}) %all-to-all-start) | async-done | bytes 524320 | tf_op jit(solution)/shard_map/all_to_all | solution.py:415
  108.5 0.1 reduce_sum.22
  108.6 0.7 broadcast_in_dim.18
  109.3 3.7 %all-to-all-start.2 = ((bf16[32,8,512]{2,1,0:T(8,128)(2,1)}), bf16[32,8,512]{2,1,0:T(8,128)(2,1)S(1)}, u32[]{:S(2)}, u32[]{:S(2)}) async-start(bf16[32,8,512]{2,1,0:T(8,128)(2,1)} %broadcast_in_dim.18), calls=%async_computation.2 | async-start | bytes 524288 | tf_op jit(solution)/shard_map/all_to_all | solution.py:342
  113.0 4.7 %collective-permute-start.11 = (f32[16,512]{1,0:T(8,128)S(1)}, f32[16,512]{1,0:T(8,128)S(1)}, u32[]{:S(2)}, u32[]{:S(2)}) collective-permute-start(f32[16,512]{1,0:T(8,128)S(1)} %add.116), channel_id=1, source_target_pairs={{0,8},{2,10},{4,12},{6,14},{8,0},{10,2},{12,4},{14,6},{1,9},{3,11}... | collective-permute-start | bytes 98312 | tf_op jit(solution)/shard_map/ppermute | solution.py:418
  117.6 4.5 %collective-permute-done.11 = f32[16,512]{1,0:T(8,128)S(1)} collective-permute-done((f32[16,512]{1,0:T(8,128)S(1)}, f32[16,512]{1,0:T(8,128)S(1)}, u32[]{:S(2)}, u32[]{:S(2)}) %collective-permute-start.11) | collective-permute-done | bytes 32800 | tf_op jit(solution)/shard_map/ppermute | solution.py:418
  122.1 3.0 %collective-permute-start.12 = (f32[16,512]{1,0:T(8,128)S(1)}, f32[16,512]{1,0:T(8,128)S(1)}, u32[]{:S(2)}, u32[]{:S(2)}) collective-permute-start(f32[16,512]{1,0:T(8,128)S(1)} %add.117), channel_id=1, source_target_pairs={{0,1},{1,0},{2,3},{3,2},{4,5},{5,4},{6,7},{7,6},{8,9},{9,8},{10,11... | collective-permute-start | bytes 98312 | tf_op jit(solution)/shard_map/ppermute | solution.py:334
  125.1 3.2 %collective-permute-done.12 = f32[16,512]{1,0:T(8,128)S(1)} collective-permute-done((f32[16,512]{1,0:T(8,128)S(1)}, f32[16,512]{1,0:T(8,128)S(1)}, u32[]{:S(2)}, u32[]{:S(2)}) %collective-permute-start.12) | collective-permute-done | bytes 32800 | tf_op jit(solution)/shard_map/ppermute | solution.py:334
  128.2 0.6 broadcast_select_fusion
  128.9 0.0 all-to-all-done.2
  128.9 0.9 bitcast_convert_fusion
  (13 shorter events, 0.0 us)
Async XLA Ops:
  0.6 2.5 %copy-start.13 = (s32[128]{0:T(128)S(1)}, s32[128]{0:T(128)}, u32[]{:S(2)}) copy-start(s32[128]{0:T(128)} %param.23) | copy-start | bytes 1540
  0.6 2.5 %copy-start.12 = (s32[256]{0:T(256)S(1)}, s32[256]{0:T(256)}, u32[]{:S(2)}) copy-start(s32[256]{0:T(256)} %param.21) | copy-start | bytes 3076
  0.7 2.5 %copy-start.11 = (s32[128,5]{0,1:T(8,128)S(1)}, s32[128,5]{0,1:T(8,128)}, u32[]{:S(2)}) copy-start(s32[128,5]{0,1:T(8,128)} %param.22) | copy-start | bytes 7684
  0.7 2.5 %copy-start.9 = (s32[256,10]{0,1:T(8,128)S(1)}, s32[256,10]{0,1:T(8,128)}, u32[]{:S(2)}) copy-start(s32[256,10]{0,1:T(8,128)} %param.20) | copy-start | bytes 30724
  0.7 2.5 %copy-start.3 = (s32[4096,15]{0,1:T(8,128)S(1)}, s32[4096,15]{0,1:T(8,128)}, u32[]{:S(2)}) copy-start(s32[4096,15]{0,1:T(8,128)} %param.18) | copy-start | bytes 737284
  0.7 2.5 %copy-start.10 = (s32[4096]{0:T(1024)S(1)}, s32[4096]{0:T(1024)}, u32[]{:S(2)}) copy-start(s32[4096]{0:T(1024)} %param.19) | copy-start | bytes 49156
  0.7 2.5 %copy-start.5 = (bf16[256,512]{1,0:T(8,128)(2,1)S(1)}, bf16[256,512]{1,0:T(8,128)(2,1)}, u32[]{:S(2)}) copy-start(bf16[256,512]{1,0:T(8,128)(2,1)} %pre_one_hbm.3) | copy-start | bytes 786436
  0.7 2.5 %copy-start.4 = (bf16[256,512]{1,0:T(8,128)(2,1)S(1)}, bf16[256,512]{1,0:T(8,128)(2,1)}, u32[]{:S(2)}) copy-start(bf16[256,512]{1,0:T(8,128)(2,1)} %pre_two_hbm.3) | copy-start | bytes 786436
  0.7 2.5 %copy-start.8 = (bf16[128,512]{1,0:T(8,128)(2,1)S(1)}, bf16[128,512]{1,0:T(8,128)(2,1)}, u32[]{:S(2)}) copy-start(bf16[128,512]{1,0:T(8,128)(2,1)} %cotangent_hbm.3) | copy-start | bytes 393220
  0.7 2.5 %copy-start.2 = (bf16[512,512]{1,0:T(8,128)(2,1)S(1)}, bf16[512,512]{1,0:T(8,128)(2,1)}, u32[]{:S(2)}) copy-start(bf16[512,512]{1,0:T(8,128)(2,1)} %weight_two_hbm.1) | copy-start | bytes 1572868
  0.7 2.5 %copy-start.1 = (bf16[512,512]{1,0:T(8,128)(2,1)S(1)}, bf16[512,512]{1,0:T(8,128)(2,1)}, u32[]{:S(2)}) copy-start(bf16[512,512]{1,0:T(8,128)(2,1)} %weight_three_hbm.1) | copy-start | bytes 1572868
  6.7 14.8 %collective-permute-start.1 = (bf16[256,512]{1,0:T(8,128)(2,1)S(1)}, bf16[256,512]{1,0:T(8,128)(2,1)}, u32[]{:S(2)}, u32[]{:S(2)}) collective-permute-start(bf16[256,512]{1,0:T(8,128)(2,1)S(1)} %get-tuple-element.25.refs_0_), channel_id=1, source_target_pairs={{0,2},{2,4},{4,6},{6,8},{8,10},{10,12},{12,14},{14,0},{16,30},{18,... | collective-permute-start | bytes 786440 | tf_op jit(solution)/shard_map/ppermute | solution.py:330
  18.3 8.4 %collective-permute-start.2 = (bf16[256,512]{1,0:T(8,128)(2,1)S(1)}, bf16[256,512]{1,0:T(8,128)(2,1)}, u32[]{:S(2)}, u32[]{:S(2)}) collective-permute-start(bf16[256,512]{1,0:T(8,128)(2,1)S(1)} %get-tuple-element.25.refs_0_), channel_id=1, source_target_pairs={{0,14},{2,0},{4,2},{6,4},{8,6},{10,8},{12,10},{14,12},{16,18},{18,... | collective-permute-start | bytes 786440 | tf_op jit(solution)/shard_map/ppermute | solution.py:330
  20.2 47.3 %copy-start = (bf16[4096,256]{1,0:T(8,128)(2,1)S(1)}, bf16[4096,256]{1,0:T(8,128)(2,1)}, u32[]{:S(2)}) copy-start(bf16[4096,256]{1,0:T(8,128)(2,1)} %features_hbm.3) | copy-start | bytes 6291460
  26.7 14.3 %collective-permute-start.5 = (bf16[16,2,16,512]{3,2,1,0:T(8,128)(2,1)S(1)}, bf16[16,2,16,512]{3,2,1,0:T(8,128)(2,1)S(1)}, u32[]{:S(2)}, u32[]{:S(2)}) collective-permute-start(bf16[16,2,16,512]{3,2,1,0:T(8,128)(2,1)S(1)} %get-tuple-element.32), channel_id=1, source_target_pairs={{0,16},{16,0},{1,17},{17,1},{2,18},{18,2},{3,19},{19,3},{4,20},{20... | collective-permute-start | bytes 1572872 | tf_op jit(solution)/shard_map/ppermute | solution.py:334
  28.6 10.3 %collective-permute-start.3 = (bf16[256,512]{1,0:T(8,128)(2,1)}, bf16[256,512]{1,0:T(8,128)(2,1)}, u32[]{:S(2)}, u32[]{:S(2)}) collective-permute-start(bf16[256,512]{1,0:T(8,128)(2,1)} %collective-permute-done.1.refs_2_), channel_id=1, source_target_pairs={{0,2},{2,4},{4,6},{6,8},{8,10},{10,12},{12,14},{14,0},{16,30},{18,... | collective-permute-start | bytes 786440 | tf_op jit(solution)/shard_map/ppermute | solution.py:330
  32.3 8.7 %collective-permute-start.4 = (bf16[256,512]{1,0:T(8,128)(2,1)}, bf16[256,512]{1,0:T(8,128)(2,1)}, u32[]{:S(2)}, u32[]{:S(2)}) collective-permute-start(bf16[256,512]{1,0:T(8,128)(2,1)} %collective-permute-done.2.refs_1_), channel_id=1, source_target_pairs={{0,14},{2,0},{4,2},{6,4},{8,6},{10,8},{12,10},{14,12},{16,18},{18,... | collective-permute-start | bytes 786440 | tf_op jit(solution)/shard_map/ppermute | solution.py:330
  34.3 33.2 %collective-permute-start = (bf16[8,256,256]{2,1,0:T(8,128)(2,1)}, bf16[8,256,256]{2,1,0:T(8,128)(2,1)S(1)}, u32[]{:S(2)}, u32[]{:S(2)}) collective-permute-start(bf16[8,256,256]{2,1,0:T(8,128)(2,1)} %dynamic-slice_bitcast_fusion), channel_id=1, source_target_pairs={{0,1},{1,0},{2,3},{3,2},{4,5},{5,4},{6,7},{7,6},{8,9},{9,8},{10,11... | collective-permute-start | bytes 3145736 | tf_op jit(solution)/shard_map/ppermute | solution.py:334
  42.0 34.7 %all-to-all-start.1 = ((bf16[32,16,512]{2,1,0:T(8,128)(2,1)}), bf16[32,16,512]{2,1,0:T(8,128)(2,1)}, u32[]{:S(2)}, u32[]{:S(2)}) async-start(bf16[32,16,512]{2,1,0:T(8,128)(2,1)} %bitcast.45), calls=%async_computation.1 | async-start | bytes 1048576 | tf_op jit(solution)/shard_map/all_to_all | solution.py:397
  51.8 8.0 %collective-permute-start.6 = (bf16[256,512]{1,0:T(8,128)(2,1)}, bf16[256,512]{1,0:T(8,128)(2,1)}, u32[]{:S(2)}, u32[]{:S(2)}) collective-permute-start(bf16[256,512]{1,0:T(8,128)(2,1)} %collective-permute-done.3.refs_4_), channel_id=1, source_target_pairs={{0,2},{2,4},{4,6},{6,8},{8,10},{10,12},{12,14},{14,0},{16,30},{18,... | collective-permute-start | bytes 786440 | tf_op jit(solution)/shard_map/ppermute | solution.py:330
  54.2 10.0 %collective-permute-start.7 = (bf16[256,512]{1,0:T(8,128)(2,1)}, bf16[256,512]{1,0:T(8,128)(2,1)S(1)}, u32[]{:S(2)}, u32[]{:S(2)}) collective-permute-start(bf16[256,512]{1,0:T(8,128)(2,1)} %collective-permute-done.4.refs_3_), channel_id=1, source_target_pairs={{0,14},{2,0},{4,2},{6,4},{8,6},{10,8},{12,10},{14,12},{16,18},{18,... | collective-permute-start | bytes 786440 | tf_op jit(solution)/shard_map/ppermute | solution.py:330
  64.1 0.7 copy-start.6
  64.8 9.8 %collective-permute-start.8 = (bf16[256,512]{1,0:T(8,128)(2,1)}, bf16[256,512]{1,0:T(8,128)(2,1)}, u32[]{:S(2)}, u32[]{:S(2)}) collective-permute-start(bf16[256,512]{1,0:T(8,128)(2,1)} %collective-permute-done.6.refs_1_), channel_id=1, source_target_pairs={{0,2},{2,4},{4,6},{6,8},{8,10},{10,12},{12,14},{14,0},{16,30},{18,... | collective-permute-start | bytes 786440 | tf_op jit(solution)/shard_map/ppermute | solution.py:330
  67.5 4.2 %copy-start.7 = (bf16[256,512]{1,0:T(8,128)(2,1)S(1)}, bf16[256,512]{1,0:T(8,128)(2,1)}, u32[]{:S(2)}) copy-start(bf16[256,512]{1,0:T(8,128)(2,1)} %copy-done.6) | copy-start | bytes 786436
  76.7 31.7 %all-to-all-start = ((bf16[64,8,512]{2,1,0:T(8,128)(2,1)}), bf16[64,8,512]{2,1,0:T(8,128)(2,1)S(1)}, u32[]{:S(2)}, u32[]{:S(2)}) async-start(bf16[64,8,512]{2,1,0:T(8,128)(2,1)} %bitcast.28), calls=%async_computation | async-start | bytes 1048576 | tf_op jit(solution)/shard_map/all_to_all | solution.py:415
  90.2 5.0 %collective-permute-start.9 = (f32[16,512]{1,0:T(8,128)S(1)}, f32[16,512]{1,0:T(8,128)S(1)}, u32[]{:S(2)}, u32[]{:S(2)}) collective-permute-start(f32[16,512]{1,0:T(8,128)S(1)} %convert_reduce_fusion), channel_id=1, source_target_pairs={{0,2},{2,0},{4,6},{6,4},{8,10},{10,8},{12,14},{14,12},{1,3},{3,1},... | collective-permute-start | bytes 98312 | tf_op jit(solution)/shard_map/ppermute | solution.py:418
  95.1 6.0 %collective-permute-start.10 = (f32[16,512]{1,0:T(8,128)S(1)}, f32[16,512]{1,0:T(8,128)S(1)}, u32[]{:S(2)}, u32[]{:S(2)}) collective-permute-start(f32[16,512]{1,0:T(8,128)S(1)} %add.115), channel_id=1, source_target_pairs={{0,4},{2,6},{4,0},{6,2},{8,12},{10,14},{12,8},{14,10},{1,5},{3,7},... | collective-permute-start | bytes 98312 | tf_op jit(solution)/shard_map/ppermute | solution.py:418
  109.3 19.6 %all-to-all-start.2 = ((bf16[32,8,512]{2,1,0:T(8,128)(2,1)}), bf16[32,8,512]{2,1,0:T(8,128)(2,1)S(1)}, u32[]{:S(2)}, u32[]{:S(2)}) async-start(bf16[32,8,512]{2,1,0:T(8,128)(2,1)} %broadcast_in_dim.18), calls=%async_computation.2 | async-start | bytes 524288 | tf_op jit(solution)/shard_map/all_to_all | solution.py:342
  113.0 9.1 %collective-permute-start.11 = (f32[16,512]{1,0:T(8,128)S(1)}, f32[16,512]{1,0:T(8,128)S(1)}, u32[]{:S(2)}, u32[]{:S(2)}) collective-permute-start(f32[16,512]{1,0:T(8,128)S(1)} %add.116), channel_id=1, source_target_pairs={{0,8},{2,10},{4,12},{6,14},{8,0},{10,2},{12,4},{14,6},{1,9},{3,11}... | collective-permute-start | bytes 98312 | tf_op jit(solution)/shard_map/ppermute | solution.py:418
  122.1 6.2 %collective-permute-start.12 = (f32[16,512]{1,0:T(8,128)S(1)}, f32[16,512]{1,0:T(8,128)S(1)}, u32[]{:S(2)}, u32[]{:S(2)}) collective-permute-start(f32[16,512]{1,0:T(8,128)S(1)} %add.117), channel_id=1, source_target_pairs={{0,1},{1,0},{2,3},{3,2},{4,5},{5,4},{6,7},{7,6},{8,9},{9,8},{10,11... | collective-permute-start | bytes 98312 | tf_op jit(solution)/shard_map/ppermute | solution.py:334
